TPU v7x, 256 devices: a whole 4x4x8 slice. The times are simulated.
256 devices in a mesh: wide: 128 (over z, y, x), narrow: 2 (over core).
Axes of the slice: x: 4, y: 4, z: 8, core: 2. Of those that a mesh axis runs over, the one named last changes fastest.
Arguments:
- features: bfloat16 [512, 96, 512], P(('wide', 'narrow')), may hold values from -6 to 6
- occupancy: int32 [512, 512], P(('wide', 'narrow')), may hold values 0 or 1
- conv1_weight: bfloat16 [27, 96, 96], replicated, may hold values from -0.125 to 0.125
- conv2_weight: bfloat16 [27, 96, 96], replicated, may hold values from -0.125 to 0.125
- out_grad: bfloat16 [512, 96, 512], P(('wide', 'narrow')), may hold values from -6 to 6
- neighbour_slots: int32 [512, 27], P(('wide', 'narrow')), may hold values from 0 to 14, as said below
- send_blocks: int32 [256, 3, 2, 2], P(('wide', 'narrow')), may hold values from 0 to 2, as said below
Outputs:
- output: bfloat16 [512, 96, 512], P(('wide', 'narrow'))
- feature_grad: bfloat16 [512, 96, 512], P(('wide', 'narrow'))
- conv1_grad: float32 [27, 96, 96], replicated
- conv2_grad: float32 [27, 96, 96], replicated
Inputs may be any that keep to these rules, and one draw needn't show every extreme that they name: `neighbour_slots`: direction 13 of block t names t's own local index. A value under 2 is an own block, 14 an empty neighbour, and other values name only halo slots that the sending device fills. `send_blocks`: entry [d, g, m, c] is the local block that device d sends as slot c to the device at wide index w + g - 1 and narrow index m; 2 means none. Entries that would leave the wide axis, and those of a device to itself, are 2; every other pair of devices at most one wide step apart has slot 0 filled, and slots of one pair name distinct blocks.
All inputs are finite; a program needn't handle non-finite values. No bound on the sum of `occupancy` on one device may be relied on, other than what follows from the above.
Results may differ from a plain program's by a relative error of at most 0.0045.
Values may be sent and summed in bfloat16 or wider, within the bound.
A program may use at most 128 MiB of HBM per device.

v0:
```python
import math

import jax
import jax.numpy as jnp
from jax import lax
from jax.sharding import PartitionSpec as P


def from_behind(block, axis, distance):
    devices = range(lax.axis_size(axis))
    route = [(i - distance, i) for i in devices if i - distance in devices]
    return lax.ppermute(block, axis, route)


def for_sending(shard):
    return jax.tree.map(lambda a: a.astype(jnp.bfloat16) if a.dtype == jnp.float32 else a, shard)


def build_padded(rows):
    block_count = rows.shape[0]
    channels = rows.shape[2]
    blocks_cube = rows.reshape(block_count, 3, 3, 3, channels, 8, 8, 8)
    along_x = jnp.concatenate(
        [blocks_cube[:, 0, :, :, :, 7:8], blocks_cube[:, 1], blocks_cube[:, 2, :, :, :, 0:1]],
        axis=4,
    )
    along_y = jnp.concatenate(
        [along_x[:, 0, :, :, :, 7:8], along_x[:, 1], along_x[:, 2, :, :, :, 0:1]], axis=4
    )
    along_z = jnp.concatenate(
        [along_y[:, 0, :, :, :, 7:8], along_y[:, 1], along_y[:, 2, :, :, :, 0:1]], axis=4
    )
    return along_z.reshape(block_count, channels, 1000)


def kernel_form(weights):
    channels = weights.shape[1]
    return weights.reshape(3, 3, 3, channels, channels).transpose(3, 4, 0, 1, 2)


def forward_conv(source_table, neighbours, weights):
    padded = build_padded(source_table[neighbours])
    block_count, channels, _ = padded.shape
    cube = padded.reshape(block_count, channels, 10, 10, 10)
    result = lax.conv_general_dilated(
        cube,
        kernel_form(weights),
        (1, 1, 1),
        "VALID",
        dimension_numbers=("NCDHW", "OIDHW", "NCDHW"),
        preferred_element_type=jnp.float32,
    )
    return (result.reshape(block_count, channels, 512), cube)


def spread_back(block_grad, weights):
    block_count, channels, _ = block_grad.shape
    grad_cube = block_grad.reshape(block_count, channels, 8, 8, 8)
    flipped = kernel_form(weights)[:, :, ::-1, ::-1, ::-1]
    result = lax.conv_general_dilated(
        grad_cube,
        flipped,
        (1, 1, 1),
        ((2, 2), (2, 2), (2, 2)),
        dimension_numbers=("NCDHW", "IODHW", "NCDHW"),
        preferred_element_type=jnp.float32,
    )
    return result.reshape(block_count, channels, 1000)


def table_grads(spread, neighbours, entries, channels, voxels):
    zero_table = jnp.zeros((entries, channels, voxels), jnp.float32)
    _, pullback = jax.vjp(lambda source_table: build_padded(source_table[neighbours]), zero_table)
    return pullback(spread)[0]


def weight_grad(block_grad, cube):
    block_count, channels, _ = block_grad.shape
    grad_cube = block_grad.reshape(block_count, channels, 8, 8, 8)
    result = lax.conv_general_dilated(
        cube,
        grad_cube,
        (1, 1, 1),
        "VALID",
        dimension_numbers=("CNDHW", "IODHW", "CNDHW"),
        preferred_element_type=jnp.float32,
    )
    return result.transpose(2, 3, 4, 0, 1).reshape(27, channels, channels)


def fetch_halo(own_blocks, send_plan):
    channels, voxels = (own_blocks.shape[1], own_blocks.shape[2])
    padded_own = jnp.concatenate([own_blocks, jnp.zeros((1, channels, voxels), own_blocks.dtype)])
    outgoing = padded_own[send_plan]
    arrived = []
    for group_index in range(3):
        portion = outgoing[group_index]
        if group_index != 1:
            portion = from_behind(portion, "wide", group_index - 1)
        arrived.append(lax.all_to_all(portion, "narrow", split_axis=0, concat_axis=0, tiled=True))
    return jnp.stack(arrived).reshape(-1, channels, voxels)


def give_back(slot_grads, send_plan, block_count):
    sorted_grads = slot_grads.reshape(send_plan.shape + slot_grads.shape[1:])
    returned = []
    for group_index in range(3):
        portion = lax.all_to_all(
            sorted_grads[group_index].astype(jnp.bfloat16),
            "narrow",
            split_axis=0,
            concat_axis=0,
            tiled=True,
        ).astype(jnp.float32)
        if group_index != 1:
            portion = from_behind(for_sending(portion), "wide", 1 - group_index).astype(
                portion.dtype
            )
        returned.append(portion)
    arrived = jnp.stack(returned)
    flat_grads = arrived.reshape((-1,) + slot_grads.shape[1:])
    summed = jax.ops.segment_sum(flat_grads, send_plan.reshape(-1), num_segments=block_count + 1)
    return summed[:block_count]


def local(features, occupancy, conv1_weight, conv2_weight, out_grad, neighbour_slots, send_blocks):
    block_count, channels, voxels = features.shape
    send_plan = send_blocks[0]
    occupied = occupancy.astype(jnp.bfloat16)[:, None, :]
    occupied_float = occupancy.astype(jnp.float32)[:, None, :]
    active = features * occupied
    zero_block = jnp.zeros((1, channels, voxels), jnp.bfloat16)
    first_table = jnp.concatenate([active, fetch_halo(active, send_plan), zero_block])
    entries = first_table.shape[0]
    first_pre, first_cube = forward_conv(first_table, neighbour_slots, conv1_weight)
    hidden = (jax.nn.silu(first_pre) * occupied_float).astype(jnp.bfloat16)
    second_table = jnp.concatenate([hidden, fetch_halo(hidden, send_plan), zero_block])
    second_pre, second_cube = forward_conv(second_table, neighbour_slots, conv2_weight)
    output = ((active.astype(jnp.float32) + second_pre) * occupied_float).astype(jnp.bfloat16)
    grad_scale = 1.0 / math.sqrt(
        block_count * voxels * lax.axis_size("wide") * lax.axis_size("narrow")
    )
    masked_grad = out_grad * occupied
    second_wgrad = weight_grad(masked_grad, second_cube) * grad_scale
    hidden_table = table_grads(
        spread_back(masked_grad, conv2_weight), neighbour_slots, entries, channels, voxels
    )
    hidden_grad = hidden_table[:block_count] + give_back(
        hidden_table[block_count : entries - 1], send_plan, block_count
    )
    sigmoid_value = jax.nn.sigmoid(first_pre)
    pre_grad = (
        hidden_grad * occupied_float * sigmoid_value * (1.0 + first_pre * (1.0 - sigmoid_value))
    ).astype(jnp.bfloat16)
    first_wgrad = weight_grad(pre_grad, first_cube) * grad_scale
    input_table = table_grads(
        spread_back(pre_grad, conv1_weight), neighbour_slots, entries, channels, voxels
    )
    input_grad = (
        masked_grad.astype(jnp.float32)
        + input_table[:block_count]
        + give_back(input_table[block_count : entries - 1], send_plan, block_count)
    )
    feature_grad = (input_grad * occupied_float).astype(jnp.bfloat16)
    first_wgrad, second_wgrad = lax.psum((first_wgrad, second_wgrad), ("wide", "narrow"))
    return (output, feature_grad, first_wgrad, second_wgrad)


def solution(mesh):
    in_specs = (
        P(("wide", "narrow"), None, None),
        P(("wide", "narrow"), None),
        P(),
        P(),
        P(("wide", "narrow"), None, None),
        P(("wide", "narrow"), None),
        P(("wide", "narrow"), None, None, None),
    )
    out_specs = (P(("wide", "narrow"), None, None), P(("wide", "narrow"), None, None), P(), P())
    return jax.shard_map(local, mesh=mesh, in_specs=in_specs, out_specs=out_specs, check_vma=False)
```

profile of v0, /device:TPU:8, one launch (start us, length us, event | category | flops | bytes accessed | tf_op | source)
XLA Modules:
  0.0 609.6 jit_solution(3040998412997145849)
XLA Ops:
  19.0 7.9 %fusion.10 = f32[2,96,10,10,10]{1,0,4,3,2:T(2,128)S(1)} fusion(bf16[3,3,3,96,96]{4,3,2,1,0:T(8,128)(2,1)} %bitcast.191, bf16[2,96,8,8,8]{1,4,3,2,0:T(8,128)(2,1)S(1)} %bitcast.187), kind=kOutput, calls=%fused_computation.66 | convolution fusion | flops 509607936 | bytes 1462272 | tf_op jit(solution)/shard_map/conv_general_dilated | solution.py:60
  35.2 7.8 %pad_add_fusion.1 = f32[2,3,3,3,96,8,8,8]{4,0,7,3,6,2,5,1:T(2,128)} fusion(f32[2,1,3,3,96,1,8,8]{4,0,7,3,6,2,5,1:T(2,128)S(1)} %get-tuple-element.17, f32[2,1,3,3,96,8,8,8]{4,0,7,3,6,2,5,1:T(2,128)S(1)} %copy_bitcast_fusion.1, f32[2,1,3,3,96,1,8,8]{4,0,7,3,6,2,5,1:T(2,128)S(1)} %get-tuple-element.16), kind=kLoop, calls=%fused_computation.9 | loop fusion | flops 5308416 | bytes 15040512 | tf_op jit(solution)/shard_map/transpose(jvp())/add_any | solution.py:24
  43.1 12.1 %copy.119 = f32[2,3,3,3,96,8,8,8]{4,7,6,5,3,2,1,0:T(8,128)} copy(f32[2,3,3,3,96,8,8,8]{4,0,7,3,6,2,5,1:T(2,128)} %pad_add_fusion.1) | data formatting | bytes 21233664 | tf_op jit(solution)/shard_map/transpose(jvp())/add_any | solution.py:24
  55.2 12.7 %copy.120 = f32[54,96,512]{2,1,0:T(8,128)} copy(f32[54,96,512]{1,2,0:T(8,128)} %bitcast.155) | data formatting | bytes 21233664 | tf_op jit(solution)/shard_map/transpose(jvp())/reshape | solution.py:22
  69.8 26.7 %scatter_fusion = f32[15,96,512]{2,1,0:T(8,128)} fusion(f32[15,96,512]{2,1,0:T(8,128)} %broadcast.91.clone, s32[54]{0:T(128)S(1)} %reshape.146, f32[54,96,512]{2,1,0:T(8,128)} %copy.120), kind=kCustom, calls=%fused_computation.4 | custom fusion | flops 2654208 | bytes 31850712 | tf_op jit(solution)/shard_map/transpose(jvp())/scatter-add | solution.py:73
  115.0 5.0 collective-permute-start.5
  120.3 5.1 all_to_all.61
  125.5 5.1 all_to_all.62
  137.7 8.5 %copy.92 = bf16[54,96,512]{1,2,0:T(8,128)(2,1)} copy(bf16[54,96,512]{2,1,0:T(8,128)(2,1)} %gather_fusion.1) | data formatting | bytes 10616832 | tf_op jit(solution)/shard_map/gather | solution.py:42
  156.7 5.4 fusion.23
  165.4 5.0 scatter_fusion.1
  171.8 5.0 convolution_multiply_fusion.1
  176.7 6.7 %fusion.7 = f32[2,96,10,10,10]{1,0,4,3,2:T(2,128)S(1)} fusion(bf16[3,3,3,96,96]{4,3,2,1,0:T(8,128)(2,1)S(1)} %bitcast.154, bf16[2,96,8,8,8]{1,4,3,2,0:T(8,128)(2,1)S(1)} %bitcast.190), kind=kOutput, calls=%fused_computation.63 | convolution fusion | flops 509607936 | bytes 1462272 | tf_op jit(solution)/shard_map/conv_general_dilated | solution.py:60
  185.8 5.4 pad_add_fusion.2
  204.4 8.2 %pad_add_fusion = f32[2,3,3,3,96,8,8,8]{4,0,7,3,6,2,5,1:T(2,128)} fusion(f32[2,1,3,3,96,1,8,8]{4,0,7,3,6,2,5,1:T(2,128)S(1)} %get-tuple-element.15, f32[2,1,3,3,96,8,8,8]{4,0,7,3,6,2,5,1:T(2,128)S(1)} %copy_bitcast_fusion, f32[2,1,3,3,96,1,8,8]{4,0,7,3,6,2,5,1:T(2,128)S(1)} %get-tuple-element.14), kind=kLoop, calls=%fused_computation.8 | loop fusion | flops 5308416 | bytes 15040512 | tf_op jit(solution)/shard_map/transpose(jvp())/add_any | solution.py:24
  214.0 12.1 %copy.131 = f32[2,3,3,3,96,8,8,8]{4,7,6,5,3,2,1,0:T(8,128)} copy(f32[2,3,3,3,96,8,8,8]{4,0,7,3,6,2,5,1:T(2,128)} %pad_add_fusion) | data formatting | bytes 21233664 | tf_op jit(solution)/shard_map/transpose(jvp())/add_any | solution.py:24
  226.2 12.7 %copy.132 = f32[54,96,512]{2,1,0:T(8,128)} copy(f32[54,96,512]{1,2,0:T(8,128)} %bitcast.156) | data formatting | bytes 21233664 | tf_op jit(solution)/shard_map/transpose(jvp())/reshape | solution.py:22
  239.5 16.9 %scatter_fusion.2 = f32[15,96,512]{2,1,0:T(8,128)S(1)} fusion(f32[15,96,512]{2,1,0:T(8,128)S(1)} %broadcast.91, s32[54]{0:T(128)S(1)} %copy-done.18, f32[54,96,512]{2,1,0:T(8,128)} %copy.132), kind=kCustom, calls=%fused_computation.6 | custom fusion | flops 2654208 | bytes 31850712 | tf_op jit(solution)/shard_map/transpose(jvp())/scatter-add | solution.py:73
  272.1 6.0 collective-permute-start.7
  278.2 5.9 all_to_all.64
  284.1 5.9 all_to_all.65
  301.1 8.5 %copy.102 = bf16[54,96,512]{1,2,0:T(8,128)(2,1)} copy(bf16[54,96,512]{2,1,0:T(8,128)(2,1)} %gather_fusion.3) | data formatting | bytes 10616832 | tf_op jit(solution)/shard_map/gather | solution.py:42
  327.4 7.4 %fusion.24 = f32[2,96,8,8,8]{1,0,4,3,2:T(2,128)} fusion(bf16[2,96,10,10,10]{1,0,4,3,2:T(2,128)(2,1)} %copy-done.9, bf16[3,3,3,96,96]{4,3,2,1,0:T(8,128)(2,1)} %bitcast.192), kind=kOutput, calls=%fused_computation.102 | convolution fusion | flops 509607936 | bytes 1274880 | tf_op jit(solution)/shard_map/conv_general_dilated | solution.py:45
  347.0 251.6 %all-reduce.23.cloned.1.call-done = (f32[27,96,96]{2,1,0:T(8,128)}, f32[27,96,96]{2,1,0:T(8,128)}) async-done(((f32[27,96,96]{2,1,0:T(8,128)}, f32[27,96,96]{2,1,0:T(8,128)}), (f32[27,96,96]{2,1,0:T(8,128)}, f32[27,96,96]{2,1,0:T(8,128)})) %all-reduce.23.cloned.1.call-update) | async-done | bytes 1990672 | tf_op jit(solution)/shard_map/psum | solution.py:165
  (164 shorter events, 140.7 us)
Async XLA Ops:
  7.2 149.5 %copy-start = (bf16[27,96,96]{2,1,0:T(8,128)(2,1)S(1)}, bf16[27,96,96]{2,1,0:T(8,128)(2,1)}, u32[]{:S(2)}) copy-start(bf16[27,96,96]{2,1,0:T(8,128)(2,1)} %param.9) | copy-start | bytes 1492996
  8.0 162.4 %copy-start.13 = (f32[2,512]{1,0:T(2,128)}, f32[2,512]{1,0:T(2,128)S(1)}, u32[]{:S(2)}) copy-start(f32[2,512]{1,0:T(2,128)S(1)} %get-tuple-element.46) | copy-start | bytes 12292
  9.9 124.2 %copy-start.2 = (bf16[2,96,512]{2,1,0:T(8,128)(2,1)}, bf16[2,96,512]{2,1,0:T(8,128)(2,1)S(1)}, u32[]{:S(2)}) copy-start(bf16[2,96,512]{2,1,0:T(8,128)(2,1)S(1)} %get-tuple-element.49) | copy-start | bytes 589828
  11.6 108.7 %collective-permute-start = (bf16[2,2,96,512]{3,2,1,0:T(8,128)(2,1)}, bf16[2,2,96,512]{3,2,1,0:T(8,128)(2,1)}, u32[]{:S(2)}, u32[]{:S(2)}) collective-permute-start(bf16[2,2,96,512]{3,2,1,0:T(8,128)(2,1)} %bitcast.1), channel_id=1, source_target_pairs={{2,0},{4,2},{6,4},{8,6},{10,8},{12,10},{14,12},{16,14},{18,16},{20... | collective-permute-start | bytes 1179656 | tf_op jit(solution)/shard_map/ppermute | solution.py:12
  16.2 109.3 %collective-permute-start.1 = (bf16[2,2,96,512]{3,2,1,0:T(8,128)(2,1)S(1)}, bf16[2,2,96,512]{3,2,1,0:T(8,128)(2,1)}, u32[]{:S(2)}, u32[]{:S(2)}) collective-permute-start(bf16[2,2,96,512]{3,2,1,0:T(8,128)(2,1)S(1)} %bitcast.186), channel_id=1, source_target_pairs={{0,2},{2,4},{4,6},{6,8},{8,10},{10,12},{12,14},{14,16},{16,18},{18... | collective-permute-start | bytes 1179656 | tf_op jit(solution)/shard_map/ppermute | solution.py:12
  43.1 77.2 %copy-start.17 = (s32[54]{0:T(128)}, s32[54]{0:T(128)S(1)}, u32[]{:S(2)}) copy-start(s32[54]{0:T(128)S(1)} %reshape.146) | copy-start | bytes 652
  98.6 21.4 %copy-start.20 = (s32[1,3,2,2]{1,3,2,0:T(2,128)S(1)}, s32[1,3,2,2]{1,3,2,0:T(2,128)}, u32[]{:S(2)}) copy-start(s32[1,3,2,2]{1,3,2,0:T(2,128)} %param.13) | copy-start | bytes 148
  104.4 7.1 %all-to-all-start.8 = ((bf16[2,2,96,512]{3,2,1,0:T(8,128)(2,1)}), bf16[2,2,96,512]{3,2,1,0:T(8,128)(2,1)}, u32[]{:S(2)}, u32[]{:S(2)}) async-start(bf16[2,2,96,512]{3,2,1,0:T(8,128)(2,1)} %bitcast.58), calls=%async_computation.8 | async-start | bytes 786432 | tf_op jit(solution)/shard_map/all_to_all | solution.py:108
  108.6 53.8 %collective-permute-start.4 = (bf16[2,2,96,512]{3,2,1,0:T(8,128)(2,1)}, bf16[2,2,96,512]{3,2,1,0:T(8,128)(2,1)S(1)}, u32[]{:S(2)}, u32[]{:S(2)}) collective-permute-start(bf16[2,2,96,512]{3,2,1,0:T(8,128)(2,1)} %all_to_all.60), channel_id=1, source_target_pairs={{0,2},{2,4},{4,6},{6,8},{8,10},{10,12},{12,14},{14,16},{16,18},{18... | collective-permute-start | bytes 1179656 | tf_op jit(solution)/shard_map/ppermute | solution.py:12
  111.5 8.8 %all-to-all-start.1 = ((bf16[2,2,96,512]{3,2,1,0:T(8,128)(2,1)}), bf16[2,2,96,512]{3,2,1,0:T(8,128)(2,1)S(1)}, u32[]{:S(2)}, u32[]{:S(2)}) async-start(bf16[2,2,96,512]{3,2,1,0:T(8,128)(2,1)} %bitcast.3), calls=%async_computation.1 | async-start | bytes 786432 | tf_op jit(solution)/shard_map/all_to_all | solution.py:100
  115.0 47.3 %collective-permute-start.5 = (bf16[2,2,96,512]{3,2,1,0:T(8,128)(2,1)}, bf16[2,2,96,512]{3,2,1,0:T(8,128)(2,1)}, u32[]{:S(2)}, u32[]{:S(2)}) collective-permute-start(bf16[2,2,96,512]{3,2,1,0:T(8,128)(2,1)} %all-to-all-done.8), channel_id=1, source_target_pairs={{2,0},{4,2},{6,4},{8,6},{10,8},{12,10},{14,12},{16,14},{18,16},{20... | collective-permute-start | bytes 1179656 | tf_op jit(solution)/shard_map/ppermute | solution.py:12
  120.2 45.1 %copy-start.21 = (s32[12]{0:T(128)}, s32[12]{0:T(128)S(1)}, u32[]{:S(2)}) copy-start(s32[12]{0:T(128)S(1)} %reshape.178) | copy-start | bytes 148
  120.3 13.9 %copy-start.23 = (bf16[15]{0:T(256)(128)(2,1)}, bf16[15]{0:T(256)(128)(2,1)S(1)}, u32[]{:S(2)}) copy-start(bf16[15]{0:T(256)(128)(2,1)S(1)} %pad.106.clone) | copy-start | bytes 94
  120.3 14.1 %copy-start.19 = (s32[1024]{0:T(1024)}, s32[1024]{0:T(1024)S(1)}, u32[]{:S(2)}) copy-start(s32[1024]{0:T(1024)S(1)} %pad_clamp_fusion) | copy-start | bytes 12292
  130.6 31.8 %all-to-all-start.7 = ((bf16[2,2,96,512]{3,2,1,0:T(8,128)(2,1)}), bf16[2,2,96,512]{3,2,1,0:T(8,128)(2,1)S(1)}, u32[]{:S(2)}, u32[]{:S(2)}) async-start(bf16[2,2,96,512]{3,2,1,0:T(8,128)(2,1)} %bitcast.56), calls=%async_computation.7 | async-start | bytes 786432 | tf_op jit(solution)/shard_map/all_to_all | solution.py:108
  193.6 84.5 %collective-permute-start.2 = (bf16[2,2,96,512]{3,2,1,0:T(8,128)(2,1)}, bf16[2,2,96,512]{3,2,1,0:T(8,128)(2,1)}, u32[]{:S(2)}, u32[]{:S(2)}) collective-permute-start(bf16[2,2,96,512]{3,2,1,0:T(8,128)(2,1)} %bitcast.22), channel_id=1, source_target_pairs={{2,0},{4,2},{6,4},{8,6},{10,8},{12,10},{14,12},{16,14},{18,16},{20... | collective-permute-start | bytes 1179656 | tf_op jit(solution)/shard_map/ppermute | solution.py:12
  197.4 86.7 %collective-permute-start.3 = (bf16[2,2,96,512]{3,2,1,0:T(8,128)(2,1)}, bf16[2,2,96,512]{3,2,1,0:T(8,128)(2,1)}, u32[]{:S(2)}, u32[]{:S(2)}) collective-permute-start(bf16[2,2,96,512]{3,2,1,0:T(8,128)(2,1)} %bitcast.26), channel_id=1, source_target_pairs={{0,2},{2,4},{4,6},{6,8},{8,10},{10,12},{12,14},{14,16},{16,18},{18... | collective-permute-start | bytes 1179656 | tf_op jit(solution)/shard_map/ppermute | solution.py:12
  262.4 5.5 all-to-all-start.11
  265.9 70.9 %collective-permute-start.6 = (bf16[2,2,96,512]{3,2,1,0:T(8,128)(2,1)}, bf16[2,2,96,512]{3,2,1,0:T(8,128)(2,1)}, u32[]{:S(2)}, u32[]{:S(2)}) collective-permute-start(bf16[2,2,96,512]{3,2,1,0:T(8,128)(2,1)} %all_to_all.63), channel_id=1, source_target_pairs={{0,2},{2,4},{4,6},{6,8},{8,10},{10,12},{12,14},{14,16},{16,18},{18... | collective-permute-start | bytes 1179656 | tf_op jit(solution)/shard_map/ppermute | solution.py:12
  268.7 9.5 %all-to-all-start.4 = ((bf16[2,2,96,512]{3,2,1,0:T(8,128)(2,1)}), bf16[2,2,96,512]{3,2,1,0:T(8,128)(2,1)S(1)}, u32[]{:S(2)}, u32[]{:S(2)}) async-start(bf16[2,2,96,512]{3,2,1,0:T(8,128)(2,1)} %bitcast.24), calls=%async_computation.4 | async-start | bytes 786432 | tf_op jit(solution)/shard_map/all_to_all | solution.py:100
  272.1 22.8 %copy-start.24 = (bf16[15]{0:T(256)(128)(2,1)S(1)}, bf16[15]{0:T(256)(128)(2,1)}, u32[]{:S(2)}) copy-start(bf16[15]{0:T(256)(128)(2,1)} %copy-done.23) | copy-start | bytes 94
  272.1 64.7 %collective-permute-start.7 = (bf16[2,2,96,512]{3,2,1,0:T(8,128)(2,1)}, bf16[2,2,96,512]{3,2,1,0:T(8,128)(2,1)}, u32[]{:S(2)}, u32[]{:S(2)}) collective-permute-start(bf16[2,2,96,512]{3,2,1,0:T(8,128)(2,1)} %copy-done.10), channel_id=1, source_target_pairs={{2,0},{4,2},{6,4},{8,6},{10,8},{12,10},{14,12},{16,14},{18,16},{20... | collective-permute-start | bytes 1179656 | tf_op jit(solution)/shard_map/ppermute | solution.py:12
  290.0 46.8 %all-to-all-start.10 = ((bf16[2,2,96,512]{3,2,1,0:T(8,128)(2,1)}), bf16[2,2,96,512]{3,2,1,0:T(8,128)(2,1)S(1)}, u32[]{:S(2)}, u32[]{:S(2)}) async-start(bf16[2,2,96,512]{3,2,1,0:T(8,128)(2,1)} %bitcast.74), calls=%async_computation.10 | async-start | bytes 786432 | tf_op jit(solution)/shard_map/all_to_all | solution.py:108
  293.5 305.1 %all-reduce.23.cloned.1.call-start = ((), (), s32[]{:S(2)}) async-start(), calls=%async_computation.12 | async-start | bytes 5308416 | tf_op jit(solution)/shard_map/psum | solution.py:165
  (17 other events, 72.7 us)
Sparse Core Ops, SparseCore 0:
  327.6 270.9 all-reduce.22
where the time goes:
time: 621 us; the launch traced here: 610 us
  waiting for transfers between devices  252 us (41%)
  local copies, waits for them, and re-layouts  119 us (19%)
  other arithmetic  105 us (17%)
  starting transfers between devices  49.8 us (8%)
  matrix products  37.2 us (6%)
  blocking collectives  31.6 us (5%)
  between operations  15.3 us (2%)
    psum x1, waiting for transfers between devices, local(): lax.psum((first_wgrad, second_wgrad), ('wide', 'narrow'))  252 us
    scatter-add x2, other arithmetic, table_grads(): source_table[neighbours]  43.7 us
    ppermute x8, starting transfers between devices, from_behind(): return lax.ppermute(block, axis, route)  28.2 us
    reshape x2, local copies, waits for them, and re-layouts, build_padded(): blocks_cube = rows.reshape(block_count, 3, 3, 3, channels, 8, 8, 8)  25.4 us
    gather x4, local copies, waits for them, and re-layouts, forward_conv(): padded = build_padded(source_table[neighbours])  25.3 us
    add_any x2, local copies, waits for them, and re-layouts, build_padded(): blocks_cube[:, 0, :, :, :, 7:8]  24.2 us
    all_to_all x4, blocking collectives, fetch_halo(): lax.all_to_all(portion, 'narrow', split_axis=0, concat_axis=0, tiled=True)  22.1 us
    add_any x2, other arithmetic, build_padded(): blocks_cube[:, 0, :, :, :, 7:8]  15.9 us
  transfers between devices with their start and end apart: 15, of which 1 were waited for; matrix products, arithmetic and copies ran while one was open for 36% of the time, Pallas kernels for 0%

commit v1 on v0

v1 whole, which is shorter than its diff:
```python
import functools

import jax
import jax.numpy as jnp
from jax import lax
from jax.experimental import pallas as pl
from jax.experimental.pallas import tpu as pltpu
from jax.sharding import PartitionSpec as P

MESH = pl.DeviceIdType.MESH
F32 = jnp.float32
BF16 = jnp.bfloat16
C = 96
L = 128
V = 512
B = 2
SLOTS = 12
EMPTY = 14
SHELL = 320
OFFSETS = [(a, b, e) for a in (-1, 0, 1) for b in (-1, 0, 1) for e in (-1, 0, 1)]
PAIRS = [(a, b) for a in (-1, 0, 1) for b in (-1, 0, 1)]
PLACE = {-1: slice(0, 1), 0: slice(1, 9), 1: slice(9, 10)}
LAYER = {-1: slice(7, 8), 0: slice(0, 8), 1: slice(0, 1)}
ROWS = 4096
WG = 27 * C
THIRD = 1296
VMEM_LIMIT = 56 * 1024 * 1024


def direction(a, b, e):
    return 9 * (a + 1) + 3 * (b + 1) + e + 1


def depth_index(shape):
    return lax.broadcasted_iota(jnp.int32, shape, len(shape) - 2)


def roll_depth(value, shift):
    return pltpu.roll(value, shift % 8, value.ndim - 2)


def to_rows(value):
    wide = jnp.concatenate([value, jnp.zeros((L - C, V), F32)], axis=0)
    return wide.T


def pack_shell(table, entry, shell, once):
    shell[0:8] = table[entry, 0]
    shell[8:16] = table[entry, 7]
    shell[16:22] = table[entry, 1:7, 0]
    shell[22:28] = table[entry, 1:7, 7]
    for at, z in ((28, 0), (34, 7)):
        plane = table[entry, 1:7, :, z, :]
        if once:
            y = depth_index(plane.shape)
            plane = jnp.where((y > 0) & (y < 7), plane, 0.0)
        shell[at : at + 6] = plane
    return shell[...].reshape(SHELL, L).astype(BF16)


def unpack_shell(rows, table, entry):
    shell = rows.astype(F32).reshape(SHELL // 8, 8, L)
    table[entry, 0] = shell[0:8]
    table[entry, 7] = shell[8:16]
    table[entry, 1:7, 0] = shell[16:22]
    table[entry, 1:7, 7] = shell[22:28]
    table[entry, 1:7, :, 0, :] = shell[28:34]
    table[entry, 1:7, :, 7, :] = shell[34:40]


def add_shell(rows, table, entry):
    shell = rows.astype(F32).reshape(SHELL // 8, 8, L)
    table[entry, 0] += shell[0:8]
    table[entry, 7] += shell[8:16]
    table[entry, 1:7, 0] += shell[16:22]
    table[entry, 1:7, 7] += shell[22:28]
    table[entry, 1:7, :, 0, :] += shell[28:34]
    table[entry, 1:7, :, 7, :] += shell[34:40]


def pack_sends(plan, table, shell, both, out):
    for t in range(B):
        both[t] = pack_shell(table, t, shell, False)

    def one(j, carry):
        out[j] = both[jnp.minimum(plan[j], B - 1)]
        return carry

    lax.fori_loop(0, SLOTS, one, 0)


def pack_gradients(grads, shell, out):
    def one(j, carry):
        out[j] = pack_shell(grads, B + j, shell, True)
        return carry

    lax.fori_loop(0, SLOTS, one, 0)


def fill_table(table, own, halo):
    for t in range(B):
        table[t] = own[t].astype(F32).reshape(8, 8, 8, L)

    def one(j, carry):
        unpack_shell(halo[j], table, B + j)
        return carry

    lax.fori_loop(0, SLOTS, one, 0)
    table[EMPTY] = jnp.zeros((8, 8, 8, L), F32)


def build_columns(slots, table, shifted, columns):
    def one(t, carry):
        for a, b in PAIRS:
            def source(e):
                return table[slots[t, direction(a, b, e)], LAYER[a], LAYER[b]]

            here = source(0)
            z = depth_index(here.shape)
            shifted[1, PLACE[a], PLACE[b]] = here
            shifted[0, PLACE[a], PLACE[b]] = roll_depth(jnp.where(z == 7, source(-1), here), 1)
            shifted[2, PLACE[a], PLACE[b]] = roll_depth(jnp.where(z == 0, source(1), here), -1)
        rows = pl.ds(pl.multiple_of(t * V, V), V)
        for o, (a, b, e) in enumerate(OFFSETS):
            part = shifted[e + 1, a + 1 : a + 9, b + 1 : b + 9]
            columns[rows, o * L : (o + 1) * L] = part.reshape(V, L).astype(BF16)
        return carry

    lax.fori_loop(0, B, one, 0)


def side_weights(weights, side):
    side[...] = jnp.zeros_like(side)
    for o in range(27):
        side[0:C, o * L : o * L + C] = weights[o]


def back_weights(weights, back):
    back[...] = jnp.zeros_like(back)
    for o in range(27):
        k, e = o // 3, o % 3
        back[k * L : k * L + C, e * L : e * L + C] = weights[o]


def spread(slots, padded, around, back, grads):
    grads[...] = jnp.zeros_like(grads)

    def one(t, carry):
        for k, (a, b) in enumerate(PAIRS):
            part = padded[t, 1 - a : 11 - a, 1 - b : 11 - b]
            around[:, k * L : (k + 1) * L] = part.reshape(800, L).astype(BF16)
        by_depth = jnp.dot(around[...], back[...], preferred_element_type=F32).reshape(10, 10, 8, 3 * L)
        low = roll_depth(by_depth[..., 0:L], -1)
        high = roll_depth(by_depth[..., 2 * L : 3 * L], 1)
        z = depth_index(low.shape)
        parts = {
            -1: jnp.where(z == 7, low, 0.0),
            0: by_depth[..., L : 2 * L] + jnp.where(z != 0, high, 0.0) + jnp.where(z != 7, low, 0.0),
            1: jnp.where(z == 0, high, 0.0),
        }
        for a, b, e in OFFSETS:
            entry = slots[t, direction(a, b, e)]
            grads[entry, LAYER[a], LAYER[b]] += parts[e][PLACE[a], PLACE[b]]
        return carry

    lax.fori_loop(0, B, one, 0)


def first_kernel(slots, plan, features, occupancy, out_grad, weights,
                 active, mask, send_active, send_grads, own_grads,
                 table, padded, around, back, grads, shell, both):
    padded[...] = jnp.zeros_like(padded)
    for t in range(B):
        seen = occupancy[t : t + 1, :].astype(F32)
        rows = to_rows(features[t].astype(F32) * seen)
        active[t] = rows.astype(BF16)
        table[t] = rows.reshape(8, 8, 8, L)
        mask[t] = jnp.broadcast_to(seen, (L, V)).T.astype(BF16)
        padded[t, 2:10, 2:10] = to_rows(out_grad[t].astype(F32) * seen).reshape(8, 8, 8, L)
    pack_sends(plan, table, shell, both, send_active)
    back_weights(weights, back)
    spread(slots, padded, around, back, grads)
    pack_gradients(grads, shell, send_grads)
    for t in range(B):
        own_grads[t] = grads[t].reshape(V, L)


def second_kernel(slots, plan, active, mask, halo, own_grads, arrived, weights,
                  hidden, send_hidden, send_grads, own_out, weight_grad,
                  table, shifted, columns, side, padded, around, back, grads, shell, both, pre):
    fill_table(table, active, halo)
    build_columns(slots, table, shifted, columns)
    side_weights(weights, side)
    for t in range(B):
        grads[t] = own_grads[t].reshape(8, 8, 8, L)

    def give(j, carry):
        add_shell(arrived[j], grads, plan[j])
        return carry

    lax.fori_loop(0, SLOTS, give, 0)
    padded[...] = jnp.zeros_like(padded)
    for t in range(B):
        value = lax.dot_general(
            columns[t * V : (t + 1) * V, :], side[...], (((1,), (1,)), ((), ())), preferred_element_type=F32
        )
        seen = mask[t].astype(F32)
        gate = jax.nn.sigmoid(value)
        out = (value * gate * seen).astype(BF16)
        hidden[t] = out
        table[t] = out.astype(F32).reshape(8, 8, 8, L)
        grad = grads[t].reshape(V, L) * seen * gate * (1.0 + value * (1.0 - gate))
        padded[t, 2:10, 2:10] = grad.reshape(8, 8, 8, L)
        pre[:, t * V : (t + 1) * V] = grad.T.astype(BF16)
    pack_sends(plan, table, shell, both, send_hidden)
    back_weights(weights, back)
    spread(slots, padded, around, back, grads)
    pack_gradients(grads, shell, send_grads)
    for t in range(B):
        own_out[t] = grads[t].reshape(V, L)
    weight_sums(pre, columns, weight_grad, 0)


def weight_sums(left, columns, out, at):
    for o in range(0, 27, 3):
        sums = jnp.dot(left[...], columns[:, o * L : (o + 3) * L], preferred_element_type=F32)
        for i in range(3):
            row = at + (o + i) * C
            out[row : row + C] = sums[0:C, i * L : (i + 1) * L]


def third_kernel(slots, plan, hidden, halo, own_grads, arrived, features, occupancy, out_grad, weights, first_sums,
                 output, feature_grad, packed,
                 table, shifted, columns, side, grads, masked, sums):
    fill_table(table, hidden, halo)
    build_columns(slots, table, shifted, columns)
    side_weights(weights, side)
    for t in range(B):
        grads[t] = own_grads[t].reshape(8, 8, 8, L)

    def give(j, carry):
        add_shell(arrived[j], grads, plan[j])
        return carry

    lax.fori_loop(0, SLOTS, give, 0)
    for t in range(B):
        seen = occupancy[t : t + 1, :].astype(F32)
        value = lax.dot_general(
            side[...], columns[t * V : (t + 1) * V, :], (((1,), (1,)), ((), ())), preferred_element_type=F32
        )
        output[t] = ((features[t].astype(F32) * seen + value[0:C]) * seen).astype(BF16)
        own = out_grad[t].astype(F32) * seen
        masked[0:C, t * V : (t + 1) * V] = own.astype(BF16)
        back = grads[t].reshape(V, L).T
        feature_grad[t] = ((own + back[0:C]) * seen).astype(BF16)
    masked[C:L] = jnp.zeros((L - C, B * V), BF16)
    sums[0:WG] = first_sums[...]
    weight_sums(masked, columns, sums, WG)
    last = sums[3 * THIRD : 4 * THIRD]
    lane = lax.broadcasted_iota(jnp.int32, (THIRD, L), 1)
    for i in range(3):
        moved = pltpu.roll(last, C - 32 * i, 1)
        packed[i * THIRD : (i + 1) * THIRD] = jnp.where(lane < C, sums[i * THIRD : (i + 1) * THIRD], moved)
    packed[3 * THIRD : ROWS] = jnp.zeros((ROWS - 3 * THIRD, L), F32)


def last_kernel(scale, packed, first, second):
    lane = lax.broadcasted_iota(jnp.int32, (THIRD, L), 1)
    last = jnp.zeros((THIRD, L), F32)
    for i in range(3):
        part = packed[i * THIRD : (i + 1) * THIRD].astype(F32) * scale
        last = jnp.where(lane // 32 == i, pltpu.roll(part, 32 + 32 * i, 1), last)
    for r in range(0, 2 * WG, 48):
        out, o, at = (first, r // C, r % C) if r < WG else (second, (r - WG) // C, r % C)
        if r < 3 * THIRD:
            rows = packed[r : r + 48].astype(F32) * scale
        else:
            rows = last[r - 3 * THIRD : r - 3 * THIRD + 48]
        out[o, at : at + 48, :] = rows[:, 0:C]


def exchange_kernel(n_wide, send_near, send_back, near, returned, send_sem, recv_sem):
    w, n = lax.axis_index("wide"), lax.axis_index("narrow")
    ahead, behind = lax.rem(w + 1, n_wide), lax.rem(w + n_wide - 1, n_wide)
    peers = [(behind, 0), (behind, 1), (ahead, 0), (ahead, 1), (w, 1 - n)]
    barrier = pltpu.get_barrier_semaphore()
    for peer in peers:
        pl.semaphore_signal(barrier, inc=1, device_id=peer, device_id_type=MESH)
    pl.semaphore_wait(barrier, 5)
    copies = []
    for i, (peer, g) in enumerate(zip(peers, (0, 0, 2, 2, 1))):
        back_group = 2 - g
        for k, (source, dest, group) in enumerate(((send_near, near, g), (send_back, returned, back_group))):
            copy = pltpu.make_async_remote_copy(
                src_ref=source.at[group, peer[1]],
                dst_ref=dest.at[group, n],
                send_sem=send_sem.at[2 * i + k],
                recv_sem=recv_sem.at[group, n, k],
                device_id=peer,
                device_id_type=MESH,
            )
            copy.start()
            copies.append((copy, group, peer[1], k, dest))
    for copy, group, m, k, dest in copies:
        copy.wait_send()
        pltpu.make_async_remote_copy(
            src_ref=dest.at[group, m], dst_ref=dest.at[group, m], send_sem=send_sem.at[0],
            recv_sem=recv_sem.at[group, m, k], device_id=(w, 1 - n), device_id_type=MESH,
        ).wait_recv()


def reduce_kernel(nz, nxy, src, out, half, sums, got1, got2, got3, whole, s1, r1, s2, r2, s3, r3, s4, r4, s5, r5, s6, r6):
    w, n = lax.axis_index("wide"), lax.axis_index("narrow")
    z, xy = w // nxy, lax.rem(w, nxy)
    halves, plane = ROWS // 2, ROWS // 2 // nxy
    piece = plane // nz
    partner = (w, 1 - n)
    in_plane = [(z * nxy + lax.rem(xy + d, nxy), n) for d in range(1, nxy)]
    in_column = [(lax.rem(z + d, nz) * nxy + xy, n) for d in range(1, nz)]
    everyone = [partner] + in_plane + in_column
    barrier = pltpu.get_barrier_semaphore()
    for peer in everyone:
        pl.semaphore_signal(barrier, inc=1, device_id=peer, device_id_type=MESH)
    pl.semaphore_wait(barrier, len(everyone))

    def start(source, dest, send, recv, peer):
        copy = pltpu.make_async_remote_copy(
            src_ref=source, dst_ref=dest, send_sem=send, recv_sem=recv, device_id=peer, device_id_type=MESH
        )
        copy.start()
        return copy

    def rows(at, size):
        return pl.ds(pl.multiple_of(at, size), size)

    mine = rows(n * halves, halves)
    copy = start(src.at[rows((1 - n) * halves, halves)], got1, s1, r1, partner)
    copy.wait()
    half[...] = (src[mine, :] + got1[...]).astype(BF16)

    copies = []
    for d, peer in enumerate(in_plane):
        to = lax.rem(xy + d + 1, nxy)
        copies.append(start(half.at[rows(to * plane, plane)], got2.at[d], s2.at[d], r2.at[d], peer))
    total = half[rows(xy * plane, plane), :].astype(F32)
    for d, copy in enumerate(copies):
        copy.wait()
        total += got2[d].astype(F32)
    sums[...] = total

    copies = []
    for d, peer in enumerate(in_column):
        to = lax.rem(z + d + 1, nz)
        copies.append(start(sums.at[rows(to * piece, piece)], got3.at[d], s3.at[d], r3.at[d], peer))
    total = sums[rows(z * piece, piece), :]
    for d, copy in enumerate(copies):
        copy.wait()
        total += got3[d]
    base = n * halves + xy * plane
    own = rows(base + z * piece, piece)
    whole[own, :] = total.astype(BF16)

    copies = [start(whole.at[own], whole.at[own], s4.at[d], r4.at[d], peer) for d, peer in enumerate(in_column)]
    for copy in copies:
        copy.wait()
    own = rows(base, plane)
    copies = [start(whole.at[own], whole.at[own], s5.at[d], r5.at[d], peer) for d, peer in enumerate(in_plane)]
    across = [start(whole.at[own], whole.at[own], s6.at[0], r6.at[0], partner)]
    for d, copy in enumerate(copies):
        copy.wait()
        origin = lax.rem(xy + nxy - d - 1, nxy)
        got = rows(n * halves + origin * plane, plane)
        across.append(start(whole.at[got], whole.at[got], s6.at[d + 1], r6.at[d + 1], partner))
    for copy in across:
        copy.wait()
    out[...] = whole[...]


VMEM_SPEC = pl.BlockSpec(memory_space=pltpu.VMEM)
SMEM_SPEC = pl.BlockSpec(memory_space=pltpu.SMEM)
ANY_SPEC = pl.BlockSpec(memory_space=pl.ANY)


def shape(dims, dtype):
    return jax.ShapeDtypeStruct(dims, dtype)


def local_call(body, outs, scratch, scalars, *args):
    specs = [SMEM_SPEC] * scalars + [VMEM_SPEC] * (len(args) - scalars)
    return pl.pallas_call(
        body,
        out_shape=outs,
        in_specs=specs,
        out_specs=[VMEM_SPEC] * len(outs),
        scratch_shapes=[pltpu.VMEM(dims, dtype) for dims, dtype in scratch],
        compiler_params=pltpu.CompilerParams(vmem_limit_bytes=VMEM_LIMIT),
    )(*args)


def exchange(n_wide, collective_id, near, back):
    dims = (3, 2, 2 * SHELL, L)
    near, back = pl.pallas_call(
        functools.partial(exchange_kernel, n_wide),
        out_shape=[shape(dims, BF16)] * 2,
        in_specs=[ANY_SPEC] * 2,
        out_specs=[ANY_SPEC] * 2,
        scratch_shapes=[pltpu.SemaphoreType.DMA((10,)), pltpu.SemaphoreType.DMA((3, 2, 2))],
        compiler_params=pltpu.CompilerParams(collective_id=collective_id, has_side_effects=True),
    )(near.reshape(dims), back.reshape(dims))
    return near.reshape(SLOTS, SHELL, L), back.reshape(SLOTS, SHELL, L)


def reduce_all(nz, nxy, packed):
    dma = pltpu.SemaphoreType.DMA
    halves, plane = ROWS // 2, ROWS // 2 // nxy
    return pl.pallas_call(
        functools.partial(reduce_kernel, nz, nxy),
        out_shape=shape((ROWS, L), BF16),
        in_specs=[VMEM_SPEC],
        out_specs=VMEM_SPEC,
        scratch_shapes=[
            pltpu.VMEM((halves, L), BF16),
            pltpu.VMEM((plane, L), F32),
            pltpu.VMEM((halves, L), F32),
            pltpu.VMEM((nxy - 1, plane, L), BF16),
            pltpu.VMEM((nz - 1, plane // nz, L), F32),
            pltpu.VMEM((ROWS, L), BF16),
            dma, dma,
            dma((nxy - 1,)), dma((nxy - 1,)),
            dma((nz - 1,)), dma((nz - 1,)),
            dma((nz - 1,)), dma((nz - 1,)),
            dma((nxy - 1,)), dma((nxy - 1,)),
            dma((nxy,)), dma((nxy,)),
        ],
        compiler_params=pltpu.CompilerParams(
            collective_id=2, has_side_effects=True, vmem_limit_bytes=VMEM_LIMIT
        ),
    )(packed)


BLOCK = (8, 8, 8, L)
SHELLS = shape((SLOTS, SHELL, L), BF16)
OWN = shape((B, V, L), F32)
ROWS16 = shape((B, V, L), BF16)
TABLE = ((EMPTY + 1,) + BLOCK, F32)
GRADS = ((EMPTY + 1,) + BLOCK, F32)
OWN_GRADS = ((B + 1,) + BLOCK, F32)
PADDED = ((B, 12, 12, 8, L), F32)
AROUND = ((800, 9 * L), BF16)
BACK = ((9 * L, 3 * L), BF16)
SHIFTED = ((3, 10, 10, 8, L), F32)
COLUMNS = ((B * V, 27 * L), BF16)
SIDE = ((L, 27 * L), BF16)
SHELL32 = ((SHELL // 8, 8, L), F32)
BOTH = ((B, SHELL, L), BF16)
LEFT = ((L, B * V), BF16)


def local(nz, nxy, features, occupancy, conv1_weight, conv2_weight, out_grad, slots, send_blocks):
    n_wide = nz * nxy
    plan = send_blocks.reshape(SLOTS)
    active, mask, send_active, send_grads, own = local_call(
        first_kernel,
        [ROWS16, ROWS16, SHELLS, SHELLS, OWN],
        [((B,) + BLOCK, F32), PADDED, AROUND, BACK, GRADS, SHELL32, BOTH],
        2, slots, plan, features, occupancy, out_grad, conv2_weight,
    )
    halo, arrived = exchange(n_wide, 0, send_active, send_grads)
    hidden, send_hidden, send_grads, own, sums = local_call(
        second_kernel,
        [ROWS16, SHELLS, SHELLS, OWN, shape((WG, L), F32)],
        [TABLE, SHIFTED, COLUMNS, SIDE, PADDED, AROUND, BACK, GRADS, SHELL32, BOTH, LEFT],
        2, slots, plan, active, mask, halo, own, arrived, conv1_weight,
    )
    halo, arrived = exchange(n_wide, 1, send_hidden, send_grads)
    output, feature_grad, packed = local_call(
        third_kernel,
        [shape((B, C, V), BF16), shape((B, C, V), BF16), shape((ROWS, L), F32)],
        [TABLE, SHIFTED, COLUMNS, SIDE, OWN_GRADS, LEFT, ((2 * WG, L), F32)],
        2, slots, plan, hidden, halo, own, arrived, features, occupancy, out_grad, conv2_weight, sums,
    )
    packed = reduce_all(nz, nxy, packed)
    scale = (B * V * 2 * n_wide) ** -0.5
    first, second = local_call(
        functools.partial(last_kernel, scale),
        [shape((27, C, C), F32)] * 2, [], 0, packed,
    )
    return output, feature_grad, first, second


def solution(mesh):
    both = ("wide", "narrow")
    n_wide = mesh.shape["wide"]
    nxy = 16 if n_wide % 16 == 0 else n_wide // 2
    return jax.shard_map(
        functools.partial(local, n_wide // nxy, nxy),
        mesh=mesh,
        in_specs=(P(both, None, None), P(both, None), P(), P(), P(both, None, None), P(both, None),
                  P(both, None, None, None)),
        out_specs=(P(both, None, None), P(both, None, None), P(), P()),
        check_vma=False,
    )
```

time: 621 us -> 124 us (0.20)
  the two profiles are of different devices: /device:TPU:8 before, /device:TPU:1 now
where the time goes in v1:
time: 124 us; the launch traced here: 123 us
  Pallas kernels  121 us (98%)
  local copies, waits for them, and re-layouts  1.4 us (1%)
    pallas_call x2, Pallas kernels, exchange(): pl.pallas_call(functools.partial(exchange_kernel, n_wide), out_shape=[sha...  50.1 us
    pallas_call x1, Pallas kernels, reduce_all(): pl.pallas_call(functools.partial(reduce_kernel, nz, nxy), out_shape=shape...  37.3 us
    pallas_call x4, Pallas kernels, local_call(): pl.pallas_call(body, out_shape=outs, in_specs=specs, out_specs=[VMEM_SPEC...  34 us

profile of v1, /device:TPU:1, one launch (start us, length us, event | category | flops | bytes accessed | tf_op | source)
XLA Modules:
  0.0 123.5 jit_solution(15410954277256171388)
XLA Ops:
  0.6 0.8 copy.12
  1.4 0.6 reshape.35.plan
  2.0 7.2 %shard_map.102 = (bf16[2,512,128]{2,1,0:T(8,128)(2,1)}, bf16[2,512,128]{2,1,0:T(8,128)(2,1)}, bf16[12,320,128]{2,1,0:T(8,128)(2,1)}, bf16[12,320,128]{2,1,0:T(8,128)(2,1)}, f32[2,512,128]{2,1,0:T(8,128)}) custom-call(s32[2,27]{1,0:T(2,128)} %slots.5, s32[12]{0:T(128)} %reshape.35.plan, bf16[2,96,512]{2,1,0:T(8,128)(2,1)} %features.3, s32[2,512]{1,0:T(2,128)} %occupancy.3, ...), custom_call_target="tpu_custom_call" | custom-call | tf_op jit(solution)/shard_map/pallas_call | solution.py:390
  9.2 27.7 %shard_map.103 = (bf16[3,2,640,128]{3,2,1,0:T(8,128)(2,1)}, bf16[3,2,640,128]{3,2,1,0:T(8,128)(2,1)}) custom-call(bf16[3,2,640,128]{3,2,1,0:T(8,128)(2,1)} %bitcast.14, bf16[3,2,640,128]{3,2,1,0:T(8,128)(2,1)} %bitcast.15), custom_call_target="tpu_custom_call" | custom-call | tf_op jit(solution)/shard_map/pallas_call | solution.py:402
  36.9 13.2 %shard_map.104 = (bf16[2,512,128]{2,1,0:T(8,128)(2,1)}, bf16[12,320,128]{2,1,0:T(8,128)(2,1)}, bf16[12,320,128]{2,1,0:T(8,128)(2,1)}, f32[2,512,128]{2,1,0:T(8,128)}, f32[2592,128]{1,0:T(8,128)}) custom-call(s32[2,27]{1,0:T(2,128)} %slots.5, s32[12]{0:T(128)} %reshape.35.plan, bf16[2,512,128]{2,1,0:T(8,128)(2,1)} %get-tuple-element.23.active, ...), custom_call_target="tpu_custom_call" | custom-call | tf_op jit(solution)/shard_map/pallas_call | solution.py:390
  50.1 22.4 %shard_map.105 = (bf16[3,2,640,128]{3,2,1,0:T(8,128)(2,1)}, bf16[3,2,640,128]{3,2,1,0:T(8,128)(2,1)}) custom-call(bf16[3,2,640,128]{3,2,1,0:T(8,128)(2,1)} %bitcast.12, bf16[3,2,640,128]{3,2,1,0:T(8,128)(2,1)} %bitcast.13), custom_call_target="tpu_custom_call" | custom-call | tf_op jit(solution)/shard_map/pallas_call | solution.py:402
  72.6 10.3 %shard_map.106 = (bf16[2,96,512]{2,1,0:T(8,128)(2,1)}, bf16[2,96,512]{2,1,0:T(8,128)(2,1)}, f32[4096,128]{1,0:T(8,128)}) custom-call(s32[2,27]{1,0:T(2,128)} %slots.5, s32[12]{0:T(128)} %reshape.35.plan, bf16[2,512,128]{2,1,0:T(8,128)(2,1)} %get-tuple-element.30.hidden, bf16[12,320,128]{2,1,0:T(8,128)(2,1)} %bitcast.8, ...), custom_call_target="tpu_custom_call" | custom-call | tf_op jit(solution)/shard_map/pallas_call | solution.py:390
  82.9 37.3 %shard_map.107.packed = bf16[4096,128]{1,0:T(8,128)(2,1)} custom-call(f32[4096,128]{1,0:T(8,128)} %get-tuple-element.39.src), custom_call_target="tpu_custom_call" | custom-call | tf_op jit(solution)/shard_map/pallas_call | solution.py:416
  120.1 3.3 %shard_map.108 = (f32[27,96,96]{2,1,0:T(8,128)}, f32[27,96,96]{2,1,0:T(8,128)}) custom-call(bf16[4096,128]{1,0:T(8,128)(2,1)} %shard_map.107.packed), custom_call_target="tpu_custom_call" | custom-call | tf_op jit(solution)/shard_map/pallas_call | solution.py:390

commit v2 on v1

v2 whole, which is shorter than its diff:
```python
import functools

import jax
import jax.numpy as jnp
from jax import lax
from jax.experimental import pallas as pl
from jax.experimental.pallas import tpu as pltpu
from jax.sharding import PartitionSpec as P

MESH = pl.DeviceIdType.MESH
F32 = jnp.float32
BF16 = jnp.bfloat16
C = 96
L = 128
V = 512
B = 2
SLOTS = 12
EMPTY = 14
SHELL = 320
OFFSETS = [(a, b, e) for a in (-1, 0, 1) for b in (-1, 0, 1) for e in (-1, 0, 1)]
PAIRS = [(a, b) for a in (-1, 0, 1) for b in (-1, 0, 1)]
PLACE = {-1: slice(0, 1), 0: slice(1, 9), 1: slice(9, 10)}
LAYER = {-1: slice(7, 8), 0: slice(0, 8), 1: slice(0, 1)}
ROWS = 2048
WG = 27 * C
QUARTER = WG // 4
MESSAGE = 2 * SHELL + 16
VMEM_LIMIT = 56 * 1024 * 1024


def direction(a, b, e):
    return 9 * (a + 1) + 3 * (b + 1) + e + 1


def depth_index(shape):
    return lax.broadcasted_iota(jnp.int32, shape, len(shape) - 2)


def roll_depth(value, shift):
    return pltpu.roll(value, shift % 8, value.ndim - 2)


def to_rows(value):
    wide = jnp.concatenate([value, jnp.zeros((L - C, V), F32)], axis=0)
    return wide.T


def pack_shell(table, entry, shell, once):
    shell[0:8] = table[entry, 0]
    shell[8:16] = table[entry, 7]
    shell[16:22] = table[entry, 1:7, 0]
    shell[22:28] = table[entry, 1:7, 7]
    for at, z in ((28, 0), (34, 7)):
        plane = table[entry, 1:7, :, z, :]
        if once:
            y = depth_index(plane.shape)
            plane = jnp.where((y > 0) & (y < 7), plane, 0.0)
        shell[at : at + 6] = plane
    return shell[...]


def unpack_shell(shell, table, entry):
    table[entry, 0] = shell[0:8]
    table[entry, 7] = shell[8:16]
    table[entry, 1:7, 0] = shell[16:22]
    table[entry, 1:7, 7] = shell[22:28]
    table[entry, 1:7, :, 0, :] = shell[28:34]
    table[entry, 1:7, :, 7, :] = shell[34:40]


def add_shell(rows, table, entry):
    shell = rows.astype(F32).reshape(SHELL // 8, 8, L)
    table[entry, 0] += shell[0:8]
    table[entry, 7] += shell[8:16]
    table[entry, 1:7, 0] += shell[16:22]
    table[entry, 1:7, 7] += shell[22:28]
    table[entry, 1:7, :, 0, :] += shell[28:34]
    table[entry, 1:7, :, 7, :] += shell[34:40]


def pack_own(table, shell, out):
    for t in range(B):
        out[t * SHELL : (t + 1) * SHELL] = pack_shell(table, t, shell, False).reshape(SHELL, L).astype(BF16)


def pack_gradients(grads, shell, out):
    def one(j, carry):
        out[j] = pack_shell(grads, B + j, shell, True).reshape(SHELL, L).astype(BF16)
        return carry

    lax.fori_loop(0, SLOTS, one, 0)


def gather_gradients(grads, chosen, shell, out):
    def one(source, carry):
        sums = [0.0, 0.0]
        for c in range(2):
            slot = 2 * source + c
            part = pack_shell(grads, B + slot, shell, True)
            sums = [total + jnp.where(chosen[slot] == float(t), part, 0.0) for t, total in enumerate(sums)]
        for t in range(B):
            out[source, t * SHELL : (t + 1) * SHELL] = sums[t].reshape(SHELL, L).astype(BF16)
        return carry

    lax.fori_loop(0, SLOTS // 2, one, 0)


def own_entries(table, own):
    for t in range(B):
        table[t] = own[t].astype(F32).reshape(8, 8, 8, L)
    table[EMPTY] = jnp.zeros((8, 8, 8, L), F32)


def halo_entries(table, halo, chosen, sources):
    for source in sources:
        blocks = [halo[source, t * SHELL : (t + 1) * SHELL].astype(F32).reshape(SHELL // 8, 8, L) for t in range(B)]
        for c in range(2):
            slot = 2 * source + c
            unpack_shell(jnp.where(chosen[slot] == 0.0, blocks[0], blocks[1]), table, B + slot)


def build_columns(slots, table, shifted, columns):
    def one(t, carry):
        for a, b in PAIRS:
            def source(e):
                return table[slots[t, direction(a, b, e)], LAYER[a], LAYER[b]]

            here = source(0)
            z = depth_index(here.shape)
            shifted[1, PLACE[a], PLACE[b]] = here
            shifted[0, PLACE[a], PLACE[b]] = roll_depth(jnp.where(z == 7, source(-1), here), 1)
            shifted[2, PLACE[a], PLACE[b]] = roll_depth(jnp.where(z == 0, source(1), here), -1)
        rows = pl.ds(pl.multiple_of(t * V, V), V)
        for o, (a, b, e) in enumerate(OFFSETS):
            part = shifted[e + 1, a + 1 : a + 9, b + 1 : b + 9]
            columns[rows, o * L : (o + 1) * L] = part.reshape(V, L).astype(BF16)
        return carry

    lax.fori_loop(0, B, one, 0)


def side_weights(weights, side):
    side[...] = jnp.zeros_like(side)
    for o in range(27):
        side[0:C, o * L : o * L + C] = weights[o]


def back_weights(weights, back):
    back[...] = jnp.zeros_like(back)
    for o in range(27):
        k, e = o // 3, o % 3
        back[k * L : k * L + C, e * L : e * L + C] = weights[o]


def spread(slots, padded, around, back, grads):
    grads[...] = jnp.zeros_like(grads)

    def one(t, carry):
        for k, (a, b) in enumerate(PAIRS):
            part = padded[t, 1 - a : 11 - a, 1 - b : 11 - b]
            around[:, k * L : (k + 1) * L] = part.reshape(800, L).astype(BF16)
        by_depth = jnp.dot(around[...], back[...], preferred_element_type=F32).reshape(10, 10, 8, 3 * L)
        low = roll_depth(by_depth[..., 0:L], -1)
        high = roll_depth(by_depth[..., 2 * L : 3 * L], 1)
        z = depth_index(low.shape)
        parts = {
            -1: jnp.where(z == 7, low, 0.0),
            0: by_depth[..., L : 2 * L] + jnp.where(z != 0, high, 0.0) + jnp.where(z != 7, low, 0.0),
            1: jnp.where(z == 0, high, 0.0),
        }
        for a, b, e in OFFSETS:
            entry = slots[t, direction(a, b, e)]
            grads[entry, LAYER[a], LAYER[b]] += parts[e][PLACE[a], PLACE[b]]
        return carry

    lax.fori_loop(0, B, one, 0)


def first_kernel(slots, plan, features, occupancy, out_grad, weights,
                 active, mask, messages, send_grads, own_grads,
                 table, padded, around, back, grads, shell):
    padded[...] = jnp.zeros_like(padded)
    for t in range(B):
        seen = occupancy[t : t + 1, :].astype(F32)
        rows = to_rows(features[t].astype(F32) * seen)
        active[t] = rows.astype(BF16)
        table[t] = rows.reshape(8, 8, 8, L)
        mask[t] = jnp.broadcast_to(seen, (L, V)).T.astype(BF16)
        padded[t, 2:10, 2:10] = to_rows(out_grad[t].astype(F32) * seen).reshape(8, 8, 8, L)
    row = lax.broadcasted_iota(jnp.int32, (16, L), 0)
    pack_own(table, shell, messages.at[0])
    for g in range(3):
        if g > 0:
            messages[g, 0 : 2 * SHELL] = messages[0, 0 : 2 * SHELL]
        rows = jnp.zeros((16, L), F32)
        for i in range(4):
            rows = jnp.where(row == i, plan[4 * g + i].astype(F32), rows)
        messages[g, 2 * SHELL : MESSAGE] = rows.astype(BF16)
    back_weights(weights, back)
    spread(slots, padded, around, back, grads)
    pack_gradients(grads, shell, send_grads)
    for t in range(B):
        own_grads[t] = grads[t].reshape(V, L)


def second_kernel(slots, plan, active, mask, halo, own_grads, arrived, weights,
                  hidden, send_hidden, send_grads, own_out, packed, chosen,
                  table, shifted, columns, side, padded, around, back, grads, shell, pre, sums):
    n = lax.axis_index("narrow")
    for source in range(SLOTS // 2):
        rows = halo[source, 2 * SHELL : MESSAGE].astype(F32)
        for c in range(2):
            row = jnp.where(n == 0, rows[c : c + 1], rows[2 + c : 3 + c])
            chosen[2 * source + c] = jnp.broadcast_to(row, (8, L))
    own_entries(table, active)
    halo_entries(table, halo, chosen, range(SLOTS // 2))
    build_columns(slots, table, shifted, columns)
    side_weights(weights, side)
    for t in range(B):
        grads[t] = own_grads[t].reshape(8, 8, 8, L)

    def give(j, carry):
        add_shell(arrived[j], grads, plan[j])
        return carry

    lax.fori_loop(0, SLOTS, give, 0)
    padded[...] = jnp.zeros_like(padded)
    for t in range(B):
        value = lax.dot_general(
            columns[t * V : (t + 1) * V, :], side[...], (((1,), (1,)), ((), ())), preferred_element_type=F32
        )
        seen = mask[t].astype(F32)
        gate = jax.nn.sigmoid(value)
        out = (value * gate * seen).astype(BF16)
        hidden[t] = out
        table[t] = out.astype(F32).reshape(8, 8, 8, L)
        grad = grads[t].reshape(V, L) * seen * gate * (1.0 + value * (1.0 - gate))
        padded[t, 2:10, 2:10] = grad.reshape(8, 8, 8, L)
        pre[:, t * V : (t + 1) * V] = grad.T.astype(BF16)
    pack_own(table, shell, send_hidden)
    back_weights(weights, back)
    spread(slots, padded, around, back, grads)
    gather_gradients(grads, chosen, shell, send_grads)
    for t in range(B):
        own_out[t] = grads[t].reshape(V, L)
    weight_sums(pre, columns, sums)
    pack_sums(sums, packed)


def weight_sums(left, columns, out):
    for o in range(0, 27, 3):
        sums = jnp.dot(left[...], columns[:, o * L : (o + 3) * L], preferred_element_type=F32)
        for i in range(3):
            row = (o + i) * C
            out[row : row + C] = sums[0:C, i * L : (i + 1) * L]


def pack_sums(sums, packed):
    last = sums[3 * QUARTER : WG]
    lane = lax.broadcasted_iota(jnp.int32, (QUARTER, L), 1)
    for i in range(3):
        moved = pltpu.roll(last, C - 32 * i, 1)
        rows = slice(i * QUARTER, (i + 1) * QUARTER)
        packed[rows] = jnp.where(lane < C, sums[rows], moved)
    packed[3 * QUARTER : ROWS] = jnp.zeros((ROWS - 3 * QUARTER, L), F32)


def last_kernel(scale, packed, first, second):
    lane = lax.broadcasted_iota(jnp.int32, (QUARTER, L), 1)
    for at, out in ((0, first), (ROWS, second)):
        whole = packed[at : at + ROWS].astype(F32) * scale
        last = jnp.zeros((QUARTER, L), F32)
        for i in range(3):
            part = whole[i * QUARTER : (i + 1) * QUARTER]
            last = jnp.where(lane // 32 == i, pltpu.roll(part, 32 + 32 * i, 1), last)
        for r in range(0, WG, 24):
            rows = whole[r : r + 24] if r < 3 * QUARTER else last[r - 3 * QUARTER : r - 3 * QUARTER + 24]
            out[r // C, r % C : r % C + 24, :] = rows[:, 0:C]


def send(source, dest, sems, peer):
    copy = pltpu.make_async_remote_copy(
        src_ref=source, dst_ref=dest, send_sem=sems[0], recv_sem=sems[1], device_id=peer, device_id_type=MESH
    )
    copy.start()
    return copy


def meet(peers):
    barrier = pltpu.get_barrier_semaphore()
    for peer in peers:
        pl.semaphore_signal(barrier, inc=1, device_id=peer, device_id_type=MESH)
    pl.semaphore_wait(barrier, len(peers))


def neighbours(n_wide):
    w, n = lax.axis_index("wide"), lax.axis_index("narrow")
    ahead, behind = lax.rem(w + 1, n_wide), lax.rem(w + n_wide - 1, n_wide)
    return w, n, ahead, behind


def exchange_kernel(n_wide, messages, send_back, near, returned, near_sems, across_sems, back_sems):
    w, n, ahead, behind = neighbours(n_wide)
    partner = (w, 1 - n)
    meet([(behind, 0), (behind, 1), (ahead, 0), (ahead, 1), partner])
    nears = [
        send(messages.at[g], near.at[g, n], (near_sems.at[0, g], near_sems.at[1, g]), peer)
        for g, peer in enumerate([(behind, n), partner, (ahead, n)])
    ]
    backs = []
    for k, (g, to, m) in enumerate([(2, behind, n), (2, behind, 1 - n), (0, ahead, n), (0, ahead, 1 - n), (1, w, 1 - n)]):
        sems = (back_sems.at[0, k], back_sems.at[1, k])
        backs.append(send(send_back.at[g, m], returned.at[g, n], sems, (to, m)))
    across = []
    for g in (0, 2):
        nears[g].wait()
        sems = (across_sems.at[0, g], across_sems.at[1, g])
        across.append(send(near.at[g, n], near.at[g, n], sems, partner))
    nears[1].wait()
    for copy in across + backs:
        copy.wait()


class Sum:
    def __init__(self, nz, nxy, src, whole, at, scratch):
        self.nz, self.nxy, self.src, self.whole, self.at = nz, nxy, src, whole, at
        (self.half, self.sums, self.fixed, self.got1, self.got2, self.got3,
         self.sem1, self.sem2, self.sem3, self.sem4, self.sem5, self.sem6) = scratch
        w, self.n = lax.axis_index("wide"), lax.axis_index("narrow")
        self.z, self.xy = w // nxy, lax.rem(w, nxy)
        self.halves, self.plane = ROWS // 2, ROWS // 2 // nxy
        self.piece = self.plane // nz
        self.partner = (w, 1 - self.n)
        self.in_plane = [(self.z * nxy + lax.rem(self.xy + d, nxy), self.n) for d in range(1, nxy)]
        self.in_column = [(lax.rem(self.z + d, nz) * nxy + self.xy, self.n) for d in range(1, nz)]

    def peers(self):
        return [self.partner] + self.in_plane + self.in_column

    def rows(self, at, size):
        return pl.ds(pl.multiple_of(at, size), size)

    def pair(self, sems, d):
        return sems.at[0, d], sems.at[1, d]

    def cores(self):
        theirs = self.src.at[self.rows((1 - self.n) * self.halves, self.halves)]
        self.copies = [send(theirs, self.got1, self.pair(self.sem1, 0), self.partner)]

    def wait(self):
        for copy in self.copies:
            copy.wait()

    def planes(self):
        self.wait()
        mine = self.src[self.rows(self.n * self.halves, self.halves), :]
        self.half[...] = (mine + self.got1[...]).astype(BF16)
        self.copies = []
        for d, peer in enumerate(self.in_plane):
            to = lax.rem(self.xy + d + 1, self.nxy)
            part = self.half.at[self.rows(to * self.plane, self.plane)]
            self.copies.append(send(part, self.got2.at[d], self.pair(self.sem2, d), peer))

    def columns(self):
        self.wait()
        total = self.half[self.rows(self.xy * self.plane, self.plane), :].astype(F32)
        for d in range(self.nxy - 1):
            total += self.got2[d].astype(F32)
        self.sums[...] = total
        self.copies = []
        for d, peer in enumerate(self.in_column):
            to = lax.rem(self.z + d + 1, self.nz)
            part = self.sums.at[self.rows(to * self.piece, self.piece)]
            self.copies.append(send(part, self.got3.at[d], self.pair(self.sem3, d), peer))

    def columns_back(self):
        self.wait()
        own = self.rows(self.z * self.piece, self.piece)
        total = self.sums[own, :]
        for d in range(self.nz - 1):
            total += self.got3[d]
        self.fixed[own, :] = total
        self.copies = [
            send(self.fixed.at[own], self.fixed.at[own], self.pair(self.sem4, d), peer)
            for d, peer in enumerate(self.in_column)
        ]

    def planes_back(self):
        self.wait()
        own = self.rows(self.at + self.n * self.halves + self.xy * self.plane, self.plane)
        self.whole[own, :] = self.fixed[...].astype(BF16)
        self.copies = [
            send(self.whole.at[own], self.whole.at[own], self.pair(self.sem5, d), peer)
            for d, peer in enumerate(self.in_plane)
        ]
        self.across = [send(self.whole.at[own], self.whole.at[own], self.pair(self.sem6, self.nxy - 1), self.partner)]

    def cores_back(self):
        for d, copy in enumerate(self.copies):
            copy.wait()
            origin = lax.rem(self.xy + self.nxy - d - 1, self.nxy)
            got = self.rows(self.at + self.n * self.halves + origin * self.plane, self.plane)
            self.across.append(send(self.whole.at[got], self.whole.at[got], self.pair(self.sem6, d), self.partner))

    def end(self):
        for copy in self.across:
            copy.wait()


def sum_scratch(nz, nxy):
    halves, plane = ROWS // 2, ROWS // 2 // nxy
    sems = [pltpu.SemaphoreType.DMA((2, count)) for count in (1, nxy - 1, nz - 1, nz - 1, nxy - 1, nxy)]
    return [
        pltpu.VMEM((halves, L), BF16),
        pltpu.VMEM((plane, L), F32),
        pltpu.VMEM((plane, L), F32),
        pltpu.VMEM((halves, L), F32),
        pltpu.VMEM((nxy - 1, plane, L), BF16),
        pltpu.VMEM((nz - 1, plane // nz, L), F32),
    ] + sems


def third_kernel(nz, nxy, slots, hidden, shells, own_grads, send_grads, features, occupancy, out_grad, weights,
                 first_packed, chosen,
                 output, feature_grad, reduced,
                 table, shifted, columns, side, grads, masked, sums, second_packed, halo, halo_grads, joined, arrived,
                 whole, halo_sems, across_sems, core_sems, back_sems, *scratch):
    n_wide = nz * nxy
    w, n, ahead, behind = neighbours(n_wide)
    partner = (w, 1 - n)
    first = Sum(nz, nxy, first_packed, whole, 0, scratch[: len(scratch) // 2])
    second = Sum(nz, nxy, second_packed, whole, ROWS, scratch[len(scratch) // 2 :])
    meet([(behind, n), (ahead, n)] + first.peers())

    def pair(sems, i):
        return sems.at[0, i], sems.at[1, i]

    nears = [
        send(shells, halo.at[g, n], pair(halo_sems, g), peer)
        for g, peer in enumerate([(behind, n), partner, (ahead, n)])
    ]
    joins = [send(send_grads.at[g, 1 - n], halo_grads.at[i], pair(core_sems, i), partner) for i, g in enumerate((0, 2))]
    backs = [send(send_grads.at[1, 1 - n], arrived.at[1], pair(back_sems, 1), partner)]
    first.cores()
    for i, g in enumerate((0, 2)):
        joins[i].wait()
        joined[i] = (send_grads[g, n].astype(F32) + halo_grads[i].astype(F32)).astype(BF16)
        backs.append(send(joined.at[i], arrived.at[g], pair(back_sems, g), ((ahead, n), (behind, n))[i]))
    first.planes()
    own_entries(table, hidden)
    side_weights(weights, side)
    for t in range(B):
        seen = occupancy[t : t + 1, :].astype(F32)
        masked[0:C, t * V : (t + 1) * V] = (out_grad[t].astype(F32) * seen).astype(BF16)
        grads[t] = own_grads[t].reshape(8, 8, 8, L)
    masked[C:L] = jnp.zeros((L - C, B * V), BF16)
    across = []
    for i, g in enumerate((0, 2)):
        nears[g].wait()
        across.append(send(halo.at[g, n], halo.at[g, n], pair(across_sems, i), partner))
    nears[1].wait()
    for copy in across:
        copy.wait()
    flat = halo.reshape(SLOTS // 2, 2 * SHELL, L)
    halo_entries(table, flat, chosen, range(SLOTS // 2))
    build_columns(slots, table, shifted, columns)
    first.columns()
    weight_sums(masked, columns, sums)
    pack_sums(sums, second_packed)
    second.cores()
    first.columns_back()
    second.planes()

    def forward(t):
        seen = occupancy[t : t + 1, :].astype(F32)
        value = lax.dot_general(
            side[...], columns[t * V : (t + 1) * V, :], (((1,), (1,)), ((), ())), preferred_element_type=F32
        )
        output[t] = ((features[t].astype(F32) * seen + value[0:C]) * seen).astype(BF16)

    forward(0)
    first.planes_back()
    forward(1)
    second.columns()
    for copy in backs:
        copy.wait()
    for t in range(B):
        for g in range(3):
            add_shell(arrived[g, t * SHELL : (t + 1) * SHELL], grads, t)
        seen = occupancy[t : t + 1, :].astype(F32)
        back = grads[t].reshape(V, L).T
        feature_grad[t] = ((out_grad[t].astype(F32) * seen + back[0:C]) * seen).astype(BF16)
    second.columns_back()
    first.cores_back()
    second.planes_back()
    first.end()
    second.cores_back()
    second.end()
    reduced[...] = whole[...]


VMEM_SPEC = pl.BlockSpec(memory_space=pltpu.VMEM)
SMEM_SPEC = pl.BlockSpec(memory_space=pltpu.SMEM)
ANY_SPEC = pl.BlockSpec(memory_space=pl.ANY)


def shape(dims, dtype):
    return jax.ShapeDtypeStruct(dims, dtype)


def local_call(body, outs, scratch, scalars, *args):
    specs = [SMEM_SPEC] * scalars + [VMEM_SPEC] * (len(args) - scalars)
    return pl.pallas_call(
        body,
        out_shape=outs,
        in_specs=specs,
        out_specs=[VMEM_SPEC] * len(outs),
        scratch_shapes=[pltpu.VMEM(dims, dtype) for dims, dtype in scratch],
        compiler_params=pltpu.CompilerParams(vmem_limit_bytes=VMEM_LIMIT),
    )(*args)


def exchange(n_wide, messages, back):
    dma = pltpu.SemaphoreType.DMA
    return pl.pallas_call(
        functools.partial(exchange_kernel, n_wide),
        out_shape=[shape((3, 2, MESSAGE, L), BF16), shape((3, 2, 2 * SHELL, L), BF16)],
        in_specs=[ANY_SPEC] * 2,
        out_specs=[ANY_SPEC] * 2,
        scratch_shapes=[dma((2, 3)), dma((2, 3)), dma((2, 5))],
        compiler_params=pltpu.CompilerParams(collective_id=0, has_side_effects=True),
    )(messages, back.reshape(3, 2, 2 * SHELL, L))


BLOCK = (8, 8, 8, L)
SHELLS = shape((SLOTS, SHELL, L), BF16)
OWN = shape((B, V, L), F32)
ROWS16 = shape((B, V, L), BF16)
TABLE = ((EMPTY + 1,) + BLOCK, F32)
GRADS = ((EMPTY + 1,) + BLOCK, F32)
OWN_GRADS = ((B + 1,) + BLOCK, F32)
PADDED = ((B, 12, 12, 8, L), F32)
AROUND = ((800, 9 * L), BF16)
BACK = ((9 * L, 3 * L), BF16)
SHIFTED = ((3, 10, 10, 8, L), F32)
COLUMNS = ((B * V, 27 * L), BF16)
SIDE = ((L, 27 * L), BF16)
SHELL32 = ((SHELL // 8, 8, L), F32)
SUMS = ((WG, L), F32)
LEFT = ((L, B * V), BF16)


def local(nz, nxy, features, occupancy, conv1_weight, conv2_weight, out_grad, slots, send_blocks):
    n_wide = nz * nxy
    dma = pltpu.SemaphoreType.DMA
    plan = send_blocks.reshape(SLOTS)
    active, mask, messages, send_grads, own = local_call(
        first_kernel,
        [ROWS16, ROWS16, shape((3, MESSAGE, L), BF16), SHELLS, OWN],
        [((B,) + BLOCK, F32), PADDED, AROUND, BACK, GRADS, SHELL32],
        2, slots, plan, features, occupancy, out_grad, conv2_weight,
    )
    halo, arrived = exchange(n_wide, messages, send_grads)
    hidden, shells, send_grads, own, packed, chosen = local_call(
        second_kernel,
        [ROWS16, shape((2 * SHELL, L), BF16), shape((SLOTS // 2, 2 * SHELL, L), BF16), OWN, shape((ROWS, L), F32),
         shape((SLOTS, 8, L), F32)],
        [TABLE, SHIFTED, COLUMNS, SIDE, PADDED, AROUND, BACK, GRADS, SHELL32, LEFT, SUMS],
        2, slots, plan, active, mask, halo.reshape(SLOTS // 2, MESSAGE, L), own, arrived.reshape(SLOTS, SHELL, L),
        conv1_weight,
    )
    scratch = [TABLE, SHIFTED, COLUMNS, SIDE, ((B,) + BLOCK, F32), LEFT, SUMS, ((ROWS, L), F32),
               ((3, 2, 2 * SHELL, L), BF16), ((2, 2 * SHELL, L), BF16), ((2, 2 * SHELL, L), BF16),
               ((3, 2 * SHELL, L), BF16), ((2 * ROWS, L), BF16)]
    output, feature_grad, reduced = pl.pallas_call(
        functools.partial(third_kernel, nz, nxy),
        out_shape=[shape((B, C, V), BF16), shape((B, C, V), BF16), shape((2 * ROWS, L), BF16)],
        in_specs=[SMEM_SPEC] + [VMEM_SPEC] * 10,
        out_specs=[VMEM_SPEC] * 3,
        scratch_shapes=[pltpu.VMEM(dims, dtype) for dims, dtype in scratch]
        + [dma((2, 3)), dma((2, 2)), dma((2, 2)), dma((2, 3))] + 2 * sum_scratch(nz, nxy),
        compiler_params=pltpu.CompilerParams(
            collective_id=1, has_side_effects=True, vmem_limit_bytes=VMEM_LIMIT
        ),
    )(slots, hidden, shells, own, send_grads.reshape(3, 2, 2 * SHELL, L), features, occupancy, out_grad, conv2_weight,
      packed, chosen)
    scale = (B * V * 2 * n_wide) ** -0.5
    first, second = local_call(
        functools.partial(last_kernel, scale),
        [shape((27, C, C), F32)] * 2, [], 0, reduced,
    )
    return output, feature_grad, first, second


def solution(mesh):
    both = ("wide", "narrow")
    n_wide = mesh.shape["wide"]
    nxy = 16 if n_wide % 16 == 0 else n_wide // 2
    return jax.shard_map(
        functools.partial(local, n_wide // nxy, nxy),
        mesh=mesh,
        in_specs=(P(both, None, None), P(both, None), P(), P(), P(both, None, None), P(both, None),
                  P(both, None, None, None)),
        out_specs=(P(both, None, None), P(both, None, None), P(), P()),
        check_vma=False,
    )
```

time: 124 us -> 105 us (0.85)
  Pallas kernels: 121 us -> 101 us
  local copies, waits for them, and re-layouts: 1.4 us -> 3.69 us
    pallas_call x2 -> x1, Pallas kernels: 50.1 us -> 24.3 us  [exchange(): pl.pallas_call(functools.partial(exchange_kernel, n_wide), out_shape=[sha...]
    pallas_call x1, Pallas kernels: 37.3 us -> 53 us  [local(): pl.pallas_call(functools.partial(third_kernel, nz, nxy), out_shape=[shape...]
    pallas_call x4 -> x3, Pallas kernels: 34 us -> 23.2 us  [local_call(): pl.pallas_call(body, out_shape=outs, in_specs=specs, out_specs=[VMEM_SPEC...]
    unnamed x1 -> x5, local copies, waits for them, and re-layouts: 0.77 us -> 3.07 us
where the time goes in v2:
time: 105 us
  Pallas kernels  101 us (96%)
  local copies, waits for them, and re-layouts  3.69 us (4%)
    pallas_call x1, Pallas kernels, local(): pl.pallas_call(functools.partial(third_kernel, nz, nxy), out_shape=[shape...  53 us
    pallas_call x1, Pallas kernels, exchange(): pl.pallas_call(functools.partial(exchange_kernel, n_wide), out_shape=[sha...  24.3 us
    pallas_call x3, Pallas kernels, local_call(): pl.pallas_call(body, out_shape=outs, in_specs=specs, out_specs=[VMEM_SPEC...  23.2 us
    unnamed x5, local copies, waits for them, and re-layouts  3.07 us

profile of v2, /device:TPU:1, one launch (start us, length us, event | category | flops | bytes accessed | tf_op | source)
XLA Modules:
  0.0 104.9 jit_solution(11609378487385203962)
XLA Ops:
  0.6 0.8 copy.12
  1.4 0.6 reshape.23.plan
  2.0 6.9 %shard_map.102 = (bf16[2,512,128]{2,1,0:T(8,128)(2,1)}, bf16[2,512,128]{2,1,0:T(8,128)(2,1)}, bf16[3,656,128]{2,1,0:T(8,128)(2,1)}, bf16[12,320,128]{2,1,0:T(8,128)(2,1)}, f32[2,512,128]{2,1,0:T(8,128)}) custom-call(s32[2,27]{1,0:T(2,128)} %slots.5, s32[12]{0:T(128)} %reshape.23.plan, bf16[2,96,512]{2,1,0:T(8,128)(2,1)} %features.3, s32[2,512]{1,0:T(2,128)} %occupancy.3, ...), custom_call_target="tpu_custom_call" | custom-call | tf_op jit(solution)/shard_map/pallas_call | solution.py:513
  8.9 24.3 %shard_map.103 = (bf16[3,2,656,128]{3,2,1,0:T(8,128)(2,1)}, bf16[3,2,640,128]{3,2,1,0:T(8,128)(2,1)}) custom-call(bf16[3,656,128]{2,1,0:T(8,128)(2,1)} %get-tuple-element.24.messages, bf16[3,2,640,128]{3,2,1,0:T(8,128)(2,1)} %bitcast.6), custom_call_target="tpu_custom_call" | custom-call | tf_op jit(solution)/shard_map/pallas_call | solution.py:525
  33.2 13.3 %shard_map.104 = (bf16[2,512,128]{2,1,0:T(8,128)(2,1)}, bf16[640,128]{1,0:T(8,128)(2,1)}, bf16[6,640,128]{2,1,0:T(8,128)(2,1)}, f32[2,512,128]{2,1,0:T(8,128)}, ...) custom-call(s32[2,27]{1,0:T(2,128)} %slots.5, s32[12]{0:T(128)} %reshape.23.plan, ...), custom_call_target="tpu_custom_call" | custom-call | tf_op jit(solution)/shard_map/pallas_call | solution.py:513
  46.5 53.0 %shard_map.105 = (bf16[2,96,512]{2,1,0:T(8,128)(2,1)}, bf16[2,96,512]{2,1,0:T(8,128)(2,1)}, bf16[4096,128]{1,0:T(8,128)(2,1)}) custom-call(s32[2,27]{1,0:T(2,128)} %slots.5, bf16[2,512,128]{2,1,0:T(8,128)(2,1)} %get-tuple-element.29.hidden, bf16[640,128]{1,0:T(8,128)(2,1)} %get-tuple-element.30.shells, f32[2,512,128]{2,1,0:T(8,128)} %get-tuple-element.31.own_grads, ...), custom_call_target="tpu_custom_call" | custom-call | tf_op jit(solution)/shard_map/pallas_call | solution.py:575
  99.5 0.0 copy-start
  99.5 3.1 %shard_map.106 = (f32[27,96,96]{2,1,0:T(8,128)}, f32[27,96,96]{2,1,0:T(8,128)}) custom-call(bf16[4096,128]{1,0:T(8,128)(2,1)} %get-tuple-element.37.packed), custom_call_target="tpu_custom_call" | custom-call | tf_op jit(solution)/shard_map/pallas_call | solution.py:513
  102.6 1.6 %copy.15 = bf16[2,96,512]{2,1,0:T(8,128)(2,1)} copy(bf16[2,96,512]{2,1,0:T(8,128)(2,1)} %get-tuple-element.44) | data formatting | bytes 393216
  104.2 0.0 copy-done
  104.2 0.7 copy.16
Async XLA Ops:
  99.5 4.7 %copy-start = (bf16[2,96,512]{2,1,0:T(8,128)(2,1)S(1)}, bf16[2,96,512]{2,1,0:T(8,128)(2,1)}, u32[]{:S(2)}) copy-start(bf16[2,96,512]{2,1,0:T(8,128)(2,1)} %get-tuple-element.45) | copy-start | bytes 589828

commit v3 on v2

v3 whole, which is shorter than its diff:
```python
import functools

import jax
import jax.numpy as jnp
from jax import lax
from jax.experimental import pallas as pl
from jax.experimental.pallas import tpu as pltpu
from jax.sharding import PartitionSpec as P

MESH = pl.DeviceIdType.MESH
F32 = jnp.float32
BF16 = jnp.bfloat16
C = 96
L = 128
V = 512
B = 2
SLOTS = 12
EMPTY = 14
SHELL = 320
OFFSETS = [(a, b, e) for a in (-1, 0, 1) for b in (-1, 0, 1) for e in (-1, 0, 1)]
PAIRS = [(a, b) for a in (-1, 0, 1) for b in (-1, 0, 1)]
PLACE = {-1: slice(0, 1), 0: slice(1, 9), 1: slice(9, 10)}
LAYER = {-1: slice(7, 8), 0: slice(0, 8), 1: slice(0, 1)}
HALF = 1024
ROWS = 2 * HALF
WG = 27 * C
QUARTER = WG // 4
MESSAGE = 2 * SHELL + 16
FACES = 384
VMEM_LIMIT = 56 * 1024 * 1024


def direction(a, b, e):
    return 9 * (a + 1) + 3 * (b + 1) + e + 1


def depth_index(shape):
    return lax.broadcasted_iota(jnp.int32, shape, len(shape) - 2)


def roll_depth(value, shift):
    return pltpu.roll(value, shift % 8, value.ndim - 2)


def to_rows(value):
    wide = jnp.concatenate([value, jnp.zeros((L - C, V), F32)], axis=0)
    return wide.T


def pack_shell(table, entry, shell):
    shell[0:8] = table[entry, 0]
    shell[8:16] = table[entry, 7]
    shell[16:22] = table[entry, 1:7, 0]
    shell[22:28] = table[entry, 1:7, 7]
    for at, z in ((28, 0), (34, 7)):
        shell[at : at + 6] = table[entry, 1:7, :, z, :]
    return shell[...].reshape(SHELL, L).astype(BF16)


def unpack_shell(shell, table, entry):
    table[entry, 0] = shell[0:8]
    table[entry, 7] = shell[8:16]
    table[entry, 1:7, 0] = shell[16:22]
    table[entry, 1:7, 7] = shell[22:28]
    table[entry, 1:7, :, 0, :] = shell[28:34]
    table[entry, 1:7, :, 7, :] = shell[34:40]


def add_faces(faces, grads, t):
    grads[t, 0] += faces[0:8]
    grads[t, 7] += faces[8:16]
    grads[t, :, 0] += faces[16:24]
    grads[t, :, 7] += faces[24:32]
    grads[t, :, :, 0, :] += faces[32:40]
    grads[t, :, :, 7, :] += faces[40:48]


def pack_own(table, shell, out):
    for t in range(B):
        out[t * SHELL : (t + 1) * SHELL] = pack_shell(table, t, shell)


def gather_gradients(faces, chosen, out):
    for g in range(3):
        for m in range(2):
            for t in range(B):
                total = 0.0
                for c in range(2):
                    slot = 4 * g + 2 * m + c
                    total += jnp.where(chosen[slot] == float(t), faces[B + slot], 0.0)
                out[g, m, t * FACES : (t + 1) * FACES] = total.reshape(FACES, L).astype(BF16)


def halo_entries(table, halo, chosen):
    for source in range(SLOTS // 2):
        blocks = [halo[source // 2, source % 2, t * SHELL : (t + 1) * SHELL].astype(F32).reshape(SHELL // 8, 8, L) for t in range(B)]
        for c in range(2):
            slot = 2 * source + c
            unpack_shell(jnp.where(chosen[slot] == 0.0, blocks[0], blocks[1]), table, B + slot)


def build_columns(slots, table, shifted, columns):
    def one(t, carry):
        for a, b in PAIRS:
            def source(e):
                return table[slots[t, direction(a, b, e)], LAYER[a], LAYER[b]]

            here = source(0)
            z = depth_index(here.shape)
            shifted[1, PLACE[a], PLACE[b]] = here
            shifted[0, PLACE[a], PLACE[b]] = roll_depth(jnp.where(z == 7, source(-1), here), 1)
            shifted[2, PLACE[a], PLACE[b]] = roll_depth(jnp.where(z == 0, source(1), here), -1)
        rows = pl.ds(pl.multiple_of(t * V, V), V)
        for o, (a, b, e) in enumerate(OFFSETS):
            part = shifted[e + 1, a + 1 : a + 9, b + 1 : b + 9]
            columns[rows, o * L : (o + 1) * L] = part.reshape(V, L).astype(BF16)
        return carry

    lax.fori_loop(0, B, one, 0)


def side_weights(weights, side):
    side[...] = jnp.zeros_like(side)
    for o in range(27):
        side[0:C, o * L : o * L + C] = weights[o]


def back_weights(weights, back):
    back[...] = jnp.zeros_like(back)
    for o in range(27):
        k, e = o // 3, o % 3
        back[k * L : k * L + C, e * L : e * L + C] = weights[o]


def spread(t, padded, around, back, middle, low, high, planes, edges):
    for k, (a, b) in enumerate(PAIRS):
        part = padded[t, 1 - a : 11 - a, 1 - b : 11 - b]
        around[:, k * L : (k + 1) * L] = part.reshape(800, L).astype(BF16)
    by_depth = jnp.dot(around[...], back[...], preferred_element_type=F32).reshape(10, 10, 8, 3 * L)
    low[...] = by_depth[..., 0:L]
    high[...] = by_depth[..., 2 * L : 3 * L]
    down = roll_depth(low[...], -1)
    up = roll_depth(high[...], 1)
    z = depth_index(up.shape)
    middle[...] = by_depth[..., L : 2 * L] + jnp.where(z != 0, up, 0.0) + jnp.where(z != 7, down, 0.0)
    y = depth_index((10, 8, L))
    for i, (source, at) in enumerate(((low, 0), (high, 7))):
        planes[i] = source[:, 1:9, at, :]
        for j, (column, row) in enumerate(((0, 7), (9, 0))):
            edge = source[:, column, at : at + 1, :]
            edges[i, j] = jnp.where(y == row, edge, 0.0)


def scatter(t, slots, middle, planes, edges, faces):
    def one(entry, carry):
        def weight(a, b, e):
            return (slots[t, direction(a, b, e)] == entry).astype(F32)

        for x, (a, px) in ((0, (1, 9)), (8, (-1, 0))):
            faces[entry, x : x + 8] += weight(a, 0, 0) * middle[px, 1:9]
            faces[entry, x] += weight(a, 1, 0) * middle[px, 9]
            faces[entry, x + 7] += weight(a, -1, 0) * middle[px, 0]
        faces[entry, 16:24] += weight(0, 1, 0) * middle[1:9, 9]
        faces[entry, 24:32] += weight(0, -1, 0) * middle[1:9, 0]
        for at, e, i in ((32, 1, 1), (40, -1, 0)):
            for a, x, px in ((0, slice(at, at + 8), slice(1, 9)), (1, at, 9), (-1, at + 7, 0)):
                total = weight(a, 0, e) * planes[i, px]
                total += weight(a, -1, e) * edges[i, 0, px] + weight(a, 1, e) * edges[i, 1, px]
                faces[entry, x] += total
        return carry

    lax.fori_loop(0, EMPTY, one, 0)


def weight_sums(left, columns, out):
    for o in range(0, 27, 3):
        sums = jnp.dot(left[...], columns[:, o * L : (o + 3) * L], preferred_element_type=F32)
        for i in range(3):
            row = (o + i) * C
            out[row : row + C] = sums[0:C, i * L : (i + 1) * L]


def pack_sums(sums, packed, at):
    last = sums[3 * QUARTER : WG]
    lane = lax.broadcasted_iota(jnp.int32, (QUARTER, L), 1)
    for i in range(3):
        moved = pltpu.roll(last, C - 32 * i, 1)
        rows = slice(i * QUARTER, (i + 1) * QUARTER)
        packed[at + i * QUARTER : at + (i + 1) * QUARTER] = jnp.where(lane < C, sums[rows], moved)
    packed[at + 3 * QUARTER : at + ROWS] = jnp.zeros((ROWS - 3 * QUARTER, L), F32)


def last_kernel(scale, packed, output, grad, output_out, grad_out, first, second):
    output_out[...] = output[...]
    grad_out[...] = grad[...]
    lane = lax.broadcasted_iota(jnp.int32, (QUARTER, L), 1)
    for at, out in ((0, first), (HALF, second)):
        parts = [packed[ROWS * n + at : ROWS * n + at + HALF] for n in range(2)]
        whole = jnp.concatenate(parts, axis=0).astype(F32) * scale
        last = jnp.zeros((QUARTER, L), F32)
        for i in range(3):
            part = whole[i * QUARTER : (i + 1) * QUARTER]
            last = jnp.where(lane // 32 == i, pltpu.roll(part, 32 + 32 * i, 1), last)
        for r in range(0, WG, 24):
            rows = whole[r : r + 24] if r < 3 * QUARTER else last[r - 3 * QUARTER : r - 3 * QUARTER + 24]
            out[r // C, r % C : r % C + 24, :] = rows[:, 0:C]


def send(source, dest, sems, peer):
    copy = pltpu.make_async_remote_copy(
        src_ref=source, dst_ref=dest, send_sem=sems[0], recv_sem=sems[1], device_id=peer, device_id_type=MESH
    )
    copy.start()
    return copy


def greet(peers):
    barrier = pltpu.get_barrier_semaphore()
    for peer in peers:
        pl.semaphore_signal(barrier, inc=1, device_id=peer, device_id_type=MESH)


def neighbours(n_wide):
    w, n = lax.axis_index("wide"), lax.axis_index("narrow")
    ahead, behind = lax.rem(w + 1, n_wide), lax.rem(w + n_wide - 1, n_wide)
    return w, n, ahead, behind


class Shells:
    def __init__(self, n_wide, halo, sems):
        self.w, self.n, ahead, behind = neighbours(n_wide)
        self.partner = (self.w, 1 - self.n)
        self.peers = [(behind, self.n), self.partner, (ahead, self.n)]
        self.halo, self.sems = halo, sems

    def start(self, sources):
        self.copies = [
            send(sources[g], self.halo.at[g, self.n], (self.sems.at[0, g], self.sems.at[1, g]), self.peers[g])
            for g in range(3)
        ]

    def finish(self):
        across = []
        for g in (0, 2):
            self.copies[g].wait()
            got = self.halo.at[g, self.n]
            across.append(send(got, got, (self.sems.at[0, 3 + g], self.sems.at[1, 3 + g]), self.partner))
        self.copies[1].wait()
        for copy in across:
            copy.wait()


class Returns:
    def __init__(self, n_wide, out, got, joined, arrived, sems):
        self.w, self.n, ahead, behind = neighbours(n_wide)
        self.partner = (self.w, 1 - self.n)
        self.to = {0: (ahead, self.n), 2: (behind, self.n)}
        self.out, self.got, self.joined, self.arrived, self.sems = out, got, joined, arrived, sems

    def pair(self, i):
        return self.sems.at[0, i], self.sems.at[1, i]

    def start(self):
        self.joins = [
            send(self.out.at[g, 1 - self.n], self.got.at[i], self.pair(i), self.partner) for i, g in enumerate((0, 2))
        ]
        self.backs = [send(self.out.at[1, 1 - self.n], self.arrived.at[1], self.pair(2), self.partner)]

    def join(self):
        for i, g in enumerate((0, 2)):
            self.joins[i].wait()
            self.joined[i] = (self.out[g, self.n].astype(F32) + self.got[i].astype(F32)).astype(BF16)
            self.backs.append(send(self.joined.at[i], self.arrived.at[g], self.pair(3 + i), self.to[g]))

    def add(self, grads):
        for copy in self.backs:
            copy.wait()
        for t in range(B):
            for g in range(3):
                faces = self.arrived[g, t * FACES : (t + 1) * FACES].astype(F32)
                add_faces(faces.reshape(FACES // 8, 8, L), grads, t)


class Sum:
    def __init__(self, nz, nxy, src, whole, scratch):
        self.nz, self.nxy, self.src, self.whole = nz, nxy, src, whole
        (self.half, self.sums, self.fixed, self.got1, self.got2, self.got3,
         self.sem1, self.sem2, self.sem3, self.sem4, self.sem5, self.sem6) = scratch
        w, self.n = lax.axis_index("wide"), lax.axis_index("narrow")
        self.z, self.xy = w // nxy, lax.rem(w, nxy)
        self.plane = ROWS // nxy
        self.piece = self.plane // nz
        self.partner = (w, 1 - self.n)
        self.in_plane = [(self.z * nxy + lax.rem(self.xy + d, nxy), self.n) for d in range(1, nxy)]
        self.in_column = [(lax.rem(self.z + d, nz) * nxy + self.xy, self.n) for d in range(1, nz)]
        self.crossing = []

    def peers(self):
        return [self.partner] + self.in_plane + self.in_column

    def rows(self, at, size):
        return pl.ds(pl.multiple_of(at, size), size)

    def pair(self, sems, d):
        return sems.at[0, d], sems.at[1, d]

    def cores(self, i):
        theirs = self.src.at[self.rows(i * ROWS + (1 - self.n) * HALF, HALF)]
        self.crossing.append(send(theirs, self.got1.at[i], self.pair(self.sem1, i), self.partner))

    def wait(self):
        for copy in self.copies:
            copy.wait()

    def planes(self):
        for i, copy in enumerate(self.crossing):
            copy.wait()
            mine = self.src[self.rows(i * ROWS + self.n * HALF, HALF), :]
            self.half[i * HALF : (i + 1) * HALF] = (mine + self.got1[i]).astype(BF16)
        self.copies = []
        for d, peer in enumerate(self.in_plane):
            to = lax.rem(self.xy + d + 1, self.nxy)
            part = self.half.at[self.rows(to * self.plane, self.plane)]
            self.copies.append(send(part, self.got2.at[d], self.pair(self.sem2, d), peer))

    def columns(self):
        self.wait()
        total = self.half[self.rows(self.xy * self.plane, self.plane), :].astype(F32)
        for d in range(self.nxy - 1):
            total += self.got2[d].astype(F32)
        self.sums[...] = total
        self.copies = []
        for d, peer in enumerate(self.in_column):
            to = lax.rem(self.z + d + 1, self.nz)
            part = self.sums.at[self.rows(to * self.piece, self.piece)]
            self.copies.append(send(part, self.got3.at[d], self.pair(self.sem3, d), peer))

    def columns_back(self):
        self.wait()
        own = self.rows(self.z * self.piece, self.piece)
        total = self.sums[own, :]
        for d in range(self.nz - 1):
            total += self.got3[d]
        self.fixed[own, :] = total
        self.copies = [
            send(self.fixed.at[own], self.fixed.at[own], self.pair(self.sem4, d), peer)
            for d, peer in enumerate(self.in_column)
        ]

    def planes_back(self):
        self.wait()
        own = self.rows(self.n * ROWS + self.xy * self.plane, self.plane)
        self.whole[own, :] = self.fixed[...].astype(BF16)
        self.copies = [
            send(self.whole.at[own], self.whole.at[own], self.pair(self.sem5, d), peer)
            for d, peer in enumerate(self.in_plane)
        ]
        self.across = [send(self.whole.at[own], self.whole.at[own], self.pair(self.sem6, self.nxy - 1), self.partner)]

    def cores_back(self):
        for d, copy in enumerate(self.copies):
            copy.wait()
            origin = lax.rem(self.xy + self.nxy - d - 1, self.nxy)
            got = self.rows(self.n * ROWS + origin * self.plane, self.plane)
            self.across.append(send(self.whole.at[got], self.whole.at[got], self.pair(self.sem6, d), self.partner))

    def end(self):
        for copy in self.across:
            copy.wait()


def sum_scratch(nz, nxy):
    plane = ROWS // nxy
    sems = [pltpu.SemaphoreType.DMA((2, count)) for count in (2, nxy - 1, nz - 1, nz - 1, nxy - 1, nxy)]
    return [
        pltpu.VMEM((ROWS, L), BF16),
        pltpu.VMEM((plane, L), F32),
        pltpu.VMEM((plane, L), F32),
        pltpu.VMEM((2, HALF, L), F32),
        pltpu.VMEM((nxy - 1, plane, L), BF16),
        pltpu.VMEM((nz - 1, plane // nz, L), F32),
    ] + sems


def main_kernel(nz, nxy, slots, plan, features, occupancy, out_grad, weights1, weights2,
                output, feature_grad, reduced,
                table, shifted, columns, side, back, around, padded, middle, low, high, planes, edges, faces, grads,
                mask, slope, chosen, shell, masked, pre, sums, packed, whole,
                messages, near, hidden_shells, hidden_near,
                out1, got1, joined1, arrived1, out2, got2, joined2, arrived2,
                near_sems, hidden_sems, back_sems1, back_sems2, *scratch):
    n_wide = nz * nxy
    n = lax.axis_index("narrow")
    actives = Shells(n_wide, near, near_sems)
    hiddens = Shells(n_wide, hidden_near, hidden_sems)
    returns1 = Returns(n_wide, out1, got1, joined1, arrived1, back_sems1)
    returns2 = Returns(n_wide, out2, got2, joined2, arrived2, back_sems2)
    total = Sum(nz, nxy, packed, whole, scratch)
    everyone = [actives.peers[0], actives.peers[2]] + total.peers()
    greet(everyone)

    for t in range(B):
        seen = occupancy[t : t + 1, :].astype(F32)
        table[t] = to_rows(features[t].astype(F32) * seen).reshape(8, 8, 8, L)
    row = lax.broadcasted_iota(jnp.int32, (16, L), 0)
    pack_own(table, shell, messages.at[0])
    for g in range(3):
        if g > 0:
            messages[g, 0 : 2 * SHELL] = messages[0, 0 : 2 * SHELL]
        rows = jnp.zeros((16, L), F32)
        for i in range(4):
            rows = jnp.where(row == i, plan[0, g, i // 2, i % 2].astype(F32), rows)
        messages[g, 2 * SHELL : MESSAGE] = rows.astype(BF16)
    pl.semaphore_wait(pltpu.get_barrier_semaphore(), len(everyone))
    actives.start([messages.at[g] for g in range(3)])

    padded[...] = jnp.zeros_like(padded)
    masked[C:L] = jnp.zeros((L - C, B * V), BF16)
    for t in range(B):
        seen = occupancy[t : t + 1, :].astype(F32)
        mask[t] = jnp.broadcast_to(seen, (L, V)).T
        own = out_grad[t].astype(F32) * seen
        masked[0:C, t * V : (t + 1) * V] = own.astype(BF16)
        padded[t, 2:10, 2:10] = to_rows(own).reshape(8, 8, 8, L)

    def transpose(weights):
        back_weights(weights, back)
        faces[...] = jnp.zeros_like(faces)

        def one(t, carry):
            spread(t, padded, around, back, middle, low, high, planes, edges)
            scatter(t, slots, middle, planes, edges, faces)
            grads[t] = middle[1:9, 1:9]
            return carry

        lax.fori_loop(0, B, one, 0)
        for t in range(B):
            add_faces(faces[t], grads, t)

    transpose(weights2)
    side_weights(weights1, side)
    table[EMPTY] = jnp.zeros((8, 8, 8, L), F32)
    actives.finish()
    for source in range(SLOTS // 2):
        rows = near[source // 2, source % 2, 2 * SHELL : MESSAGE].astype(F32)
        for c in range(2):
            row = jnp.where(n == 0, rows[c : c + 1], rows[2 + c : 3 + c])
            chosen[2 * source + c] = jnp.broadcast_to(row, (8, L))
    gather_gradients(faces, chosen, out1)
    returns1.start()

    halo_entries(table, near, chosen)
    returns1.join()
    build_columns(slots, table, shifted, columns)
    for t in range(B):
        value = lax.dot_general(
            columns[t * V : (t + 1) * V, :], side[...], (((1,), (1,)), ((), ())), preferred_element_type=F32
        )
        seen = mask[t]
        gate = jax.nn.sigmoid(value)
        table[t] = (value * gate * seen).astype(BF16).astype(F32).reshape(8, 8, 8, L)
        slope[t] = seen * gate * (1.0 + value * (1.0 - gate))
    pack_own(table, shell, hidden_shells)
    hiddens.start([hidden_shells] * 3)
    side_weights(weights2, side)
    returns1.add(grads)
    for t in range(B):
        grad = grads[t].reshape(V, L) * slope[t]
        padded[t, 2:10, 2:10] = grad.reshape(8, 8, 8, L)
        pre[:, t * V : (t + 1) * V] = grad.T.astype(BF16)
    weight_sums(pre, columns, sums)
    pack_sums(sums, packed, 0)
    total.cores(0)

    hiddens.finish()
    halo_entries(table, hidden_near, chosen)
    build_columns(slots, table, shifted, columns)
    weight_sums(masked, columns, sums)
    pack_sums(sums, packed, ROWS)
    total.cores(1)
    total.planes()
    transpose(weights1)
    gather_gradients(faces, chosen, out2)
    returns2.start()
    total.columns()
    returns2.join()

    def forward(t):
        seen = occupancy[t : t + 1, :].astype(F32)
        value = lax.dot_general(
            side[...], columns[t * V : (t + 1) * V, :], (((1,), (1,)), ((), ())), preferred_element_type=F32
        )
        output[t] = ((features[t].astype(F32) * seen + value[0:C]) * seen).astype(BF16)

    forward(0)
    total.columns_back()
    forward(1)
    total.planes_back()
    returns2.add(grads)
    for t in range(B):
        seen = occupancy[t : t + 1, :].astype(F32)
        own = grads[t].reshape(V, L).T
        feature_grad[t] = ((out_grad[t].astype(F32) * seen + own[0:C]) * seen).astype(BF16)
    total.cores_back()
    total.end()
    reduced[...] = whole[...]


VMEM_SPEC = pl.BlockSpec(memory_space=pltpu.VMEM)
SMEM_SPEC = pl.BlockSpec(memory_space=pltpu.SMEM)


def shape(dims, dtype):
    return jax.ShapeDtypeStruct(dims, dtype)


def local_call(body, outs, scratch, scalars, *args):
    specs = [SMEM_SPEC] * scalars + [VMEM_SPEC] * (len(args) - scalars)
    return pl.pallas_call(
        body,
        out_shape=outs,
        in_specs=specs,
        out_specs=[VMEM_SPEC] * len(outs),
        scratch_shapes=[pltpu.VMEM(dims, dtype) for dims, dtype in scratch],
        compiler_params=pltpu.CompilerParams(vmem_limit_bytes=VMEM_LIMIT),
    )(*args)


BLOCK = (8, 8, 8, L)
SCRATCH = [
    ((EMPTY + 1,) + BLOCK, F32),
    ((3, 10, 10, 8, L), F32),
    ((B * V, 27 * L), BF16),
    ((L, 27 * L), BF16),
    ((9 * L, 3 * L), BF16),
    ((800, 9 * L), BF16),
    ((B, 12, 12, 8, L), F32),
    ((10, 10, 8, L), F32),
    ((10, 10, 8, L), F32),
    ((10, 10, 8, L), F32),
    ((2, 10, 8, L), F32),
    ((2, 2, 10, 8, L), F32),
    ((EMPTY, FACES // 8, 8, L), F32),
    ((B,) + BLOCK, F32),
    ((B, V, L), F32),
    ((B, V, L), F32),
    ((SLOTS, 8, L), F32),
    ((SHELL // 8, 8, L), F32),
    ((L, B * V), BF16),
    ((L, B * V), BF16),
    ((WG, L), F32),
    ((2 * ROWS, L), F32),
    ((2 * ROWS, L), BF16),
    ((3, MESSAGE, L), BF16),
    ((3, 2, MESSAGE, L), BF16),
    ((2 * SHELL, L), BF16),
    ((3, 2, 2 * SHELL, L), BF16),
] + 2 * [
    ((3, 2, 2 * FACES, L), BF16),
    ((2, 2 * FACES, L), BF16),
    ((2, 2 * FACES, L), BF16),
    ((3, 2 * FACES, L), BF16),
]


def local(nz, nxy, features, occupancy, conv1_weight, conv2_weight, out_grad, slots, send_blocks):
    dma = pltpu.SemaphoreType.DMA
    blocks = shape((B, C, V), BF16)
    output, feature_grad, reduced = pl.pallas_call(
        functools.partial(main_kernel, nz, nxy),
        out_shape=[blocks, blocks, shape((2 * ROWS, L), BF16)],
        in_specs=[SMEM_SPEC] * 2 + [VMEM_SPEC] * 5,
        out_specs=[VMEM_SPEC] * 3,
        scratch_shapes=[pltpu.VMEM(dims, dtype) for dims, dtype in SCRATCH]
        + [dma((2, 6)), dma((2, 6)), dma((2, 5)), dma((2, 5))] + sum_scratch(nz, nxy),
        compiler_params=pltpu.CompilerParams(
            collective_id=0, has_side_effects=True, vmem_limit_bytes=VMEM_LIMIT
        ),
    )(slots, send_blocks, features, occupancy, out_grad, conv1_weight, conv2_weight)
    scale = (B * V * 2 * nz * nxy) ** -0.5
    return pl.pallas_call(
        functools.partial(last_kernel, scale),
        out_shape=[blocks, blocks] + [shape((27, C, C), F32)] * 2,
        in_specs=[VMEM_SPEC] * 3,
        out_specs=[VMEM_SPEC] * 4,
        compiler_params=pltpu.CompilerParams(vmem_limit_bytes=VMEM_LIMIT),
    )(reduced, output, feature_grad)


def solution(mesh):
    both = ("wide", "narrow")
    n_wide = mesh.shape["wide"]
    nxy = 16 if n_wide % 16 == 0 else n_wide // 2
    return jax.shard_map(
        functools.partial(local, n_wide // nxy, nxy),
        mesh=mesh,
        in_specs=(P(both, None, None), P(both, None), P(), P(), P(both, None, None), P(both, None),
                  P(both, None, None, None)),
        out_specs=(P(both, None, None), P(both, None, None), P(), P()),
        check_vma=False,
    )
```

time: 105 us -> 77.5 us (0.74)
  Pallas kernels: 101 us -> 75.3 us
  local copies, waits for them, and re-layouts: 3.69 us -> 1.34 us
    pallas_call x5 -> x2, Pallas kernels: 101 us -> 75.3 us  [the longest x1 71.8 us: local(): pl.pallas_call(functools.partial(main_kernel, nz, nxy), out_shape=[blocks...]
    unnamed x5 -> x1, local copies, waits for them, and re-layouts: 3.07 us -> 1.34 us
where the time goes in v3:
time: 77.5 us; the launch traced here: 77.3 us
  Pallas kernels  75.3 us (97%)
  local copies, waits for them, and re-layouts  1.34 us (2%)
    pallas_call x1, Pallas kernels, local(): pl.pallas_call(functools.partial(main_kernel, nz, nxy), out_shape=[blocks...  71.8 us
    pallas_call x1, Pallas kernels, local(): pl.pallas_call(functools.partial(last_kernel, scale), out_shape=[blocks,...  3.5 us

profile of v3, /device:TPU:1, one launch (start us, length us, event | category | flops | bytes accessed | tf_op | source)
XLA Modules:
  0.0 77.3 jit_solution(6483174481551713510)
XLA Ops:
  0.6 1.3 %copy.11.plan = s32[1,3,2,2]{3,2,1,0:T(2,128)} copy(s32[1,3,2,2]{1,3,2,0:T(2,128)} %param.13) | data formatting | bytes 96 | tf_op args[6]
  2.0 71.8 %shard_map.102 = (bf16[2,96,512]{2,1,0:T(8,128)(2,1)}, bf16[2,96,512]{2,1,0:T(8,128)(2,1)}, bf16[4096,128]{1,0:T(8,128)(2,1)}) custom-call(s32[2,27]{1,0:T(2,128)} %slots.1, s32[1,3,2,2]{3,2,1,0:T(2,128)} %copy.11.plan, bf16[2,96,512]{2,1,0:T(8,128)(2,1)} %features.1, s32[2,512]{1,0:T(2,128)} %occupancy.1, bf16[2,96,512]{2,1,0:T(8,128)(2,1)} %out_grad.1, ...), custom_call_target="tpu_custom_call" | custom-call | tf_op jit(solution)/shard_map/pallas_call | solution.py:569
  73.8 3.5 %shard_map.103 = (bf16[2,96,512]{2,1,0:T(8,128)(2,1)}, bf16[2,96,512]{2,1,0:T(8,128)(2,1)}, f32[27,96,96]{2,1,0:T(8,128)}, f32[27,96,96]{2,1,0:T(8,128)}) custom-call(bf16[4096,128]{1,0:T(8,128)(2,1)} %get-tuple-element.7.packed, bf16[2,96,512]{2,1,0:T(8,128)(2,1)} %get-tuple-element.8.output, bf16[2,96,512]{2,1,0:T(8,128)(2,1)} %get-tuple-element.9.grad), custom_call_target="tpu_custom_call" | custom-call | tf_op jit(solution)/shard_map/pallas_call | solution.py:581

commit v4 on v3

--- a/solution.py
+++ b/solution.py
@@ -17,6 +17,7 @@
 SLOTS = 12
 EMPTY = 14
 SHELL = 320
+TIGHT = SHELL * 3 // 4
 OFFSETS = [(a, b, e) for a in (-1, 0, 1) for b in (-1, 0, 1) for e in (-1, 0, 1)]
 PAIRS = [(a, b) for a in (-1, 0, 1) for b in (-1, 0, 1)]
 PLACE = {-1: slice(0, 1), 0: slice(1, 9), 1: slice(9, 10)}
@@ -25,8 +26,9 @@
 ROWS = 2 * HALF
 WG = 27 * C
 QUARTER = WG // 4
-MESSAGE = 2 * SHELL + 16
+MESSAGE = 2 * TIGHT + 16
 FACES = 384
+TIGHT_FACES = FACES * 3 // 4
 VMEM_LIMIT = 56 * 1024 * 1024
 
 
@@ -45,6 +47,25 @@
 def to_rows(value):
     wide = jnp.concatenate([value, jnp.zeros((L - C, V), F32)], axis=0)
     return wide.T
+
+
+def squeeze(rows):
+    q = rows.shape[0] // 4
+    lane = lax.broadcasted_iota(jnp.int32, (q, L), 1)
+    last = rows[3 * q :]
+    parts = [jnp.where(lane < C, rows[i * q : (i + 1) * q], pltpu.roll(last, C - 32 * i, 1)) for i in range(3)]
+    return jnp.concatenate(parts, axis=0)
+
+
+def stretch(rows):
+    q = rows.shape[0] // 3
+    lane = lax.broadcasted_iota(jnp.int32, (q, L), 1)
+    parts, last = [], jnp.zeros((q, L), F32)
+    for i in range(3):
+        part = rows[i * q : (i + 1) * q]
+        parts.append(jnp.where(lane < C, part, 0.0))
+        last = jnp.where(lane // 32 == i, pltpu.roll(part, 32 + 32 * i, 1), last)
+    return jnp.concatenate(parts + [last], axis=0)
 
 
 def pack_shell(table, entry, shell):
@@ -54,7 +75,7 @@
     shell[22:28] = table[entry, 1:7, 7]
     for at, z in ((28, 0), (34, 7)):
         shell[at : at + 6] = table[entry, 1:7, :, z, :]
-    return shell[...].reshape(SHELL, L).astype(BF16)
+    return squeeze(shell[...].reshape(SHELL, L)).astype(BF16)
 
 
 def unpack_shell(shell, table, entry):
@@ -75,9 +96,8 @@
     grads[t, :, :, 7, :] += faces[40:48]
 
 
-def pack_own(table, shell, out):
-    for t in range(B):
-        out[t * SHELL : (t + 1) * SHELL] = pack_shell(table, t, shell)
+def pack_own(table, shell, out, t):
+    out[t * TIGHT : (t + 1) * TIGHT] = pack_shell(table, t, shell)
 
 
 def gather_gradients(faces, chosen, out):
@@ -88,12 +108,15 @@
                 for c in range(2):
                     slot = 4 * g + 2 * m + c
                     total += jnp.where(chosen[slot] == float(t), faces[B + slot], 0.0)
-                out[g, m, t * FACES : (t + 1) * FACES] = total.reshape(FACES, L).astype(BF16)
+                out[g, m, t * TIGHT_FACES : (t + 1) * TIGHT_FACES] = squeeze(total.reshape(FACES, L)).astype(BF16)
 
 
 def halo_entries(table, halo, chosen):
     for source in range(SLOTS // 2):
-        blocks = [halo[source // 2, source % 2, t * SHELL : (t + 1) * SHELL].astype(F32).reshape(SHELL // 8, 8, L) for t in range(B)]
+        blocks = []
+        for t in range(B):
+            rows = halo[source // 2, source % 2, t * TIGHT : (t + 1) * TIGHT].astype(F32)
+            blocks.append(stretch(rows).reshape(SHELL // 8, 8, L))
         for c in range(2):
             slot = 2 * source + c
             unpack_shell(jnp.where(chosen[slot] == 0.0, blocks[0], blocks[1]), table, B + slot)
@@ -194,16 +217,15 @@
     output_out[...] = output[...]
     grad_out[...] = grad[...]
     lane = lax.broadcasted_iota(jnp.int32, (QUARTER, L), 1)
-    for at, out in ((0, first), (HALF, second)):
-        parts = [packed[ROWS * n + at : ROWS * n + at + HALF] for n in range(2)]
-        whole = jnp.concatenate(parts, axis=0).astype(F32) * scale
+    for i, out in enumerate((first, second)):
+        whole = packed[i * ROWS : (i + 1) * ROWS].astype(F32) * scale
         last = jnp.zeros((QUARTER, L), F32)
-        for i in range(3):
-            part = whole[i * QUARTER : (i + 1) * QUARTER]
-            last = jnp.where(lane // 32 == i, pltpu.roll(part, 32 + 32 * i, 1), last)
+        for k in range(3):
+            part = whole[k * QUARTER : (k + 1) * QUARTER]
+            last = jnp.where(lane // 32 == k, pltpu.roll(part, 32 + 32 * k, 1), last)
         for r in range(0, WG, 24):
-            rows = whole[r : r + 24] if r < 3 * QUARTER else last[r - 3 * QUARTER : r - 3 * QUARTER + 24]
-            out[r // C, r % C : r % C + 24, :] = rows[:, 0:C]
+            part = whole[r : r + 24] if r < 3 * QUARTER else last[r - 3 * QUARTER : r - 3 * QUARTER + 24]
+            out[r // C, r % C : r % C + 24, :] = part[:, 0:C]
 
 
 def send(source, dest, sems, peer):
@@ -231,22 +253,32 @@
         self.w, self.n, ahead, behind = neighbours(n_wide)
         self.partner = (self.w, 1 - self.n)
         self.peers = [(behind, self.n), self.partner, (ahead, self.n)]
-        self.halo, self.sems = halo, sems
-
-    def start(self, sources):
-        self.copies = [
-            send(sources[g], self.halo.at[g, self.n], (self.sems.at[0, g], self.sems.at[1, g]), self.peers[g])
+        self.halo, self.sems, self.copies = halo, sems, {}
+
+    def pair(self, k, i):
+        return self.sems.at[0, k, i], self.sems.at[1, k, i]
+
+    def rows(self, k):
+        return pl.ds(k * TIGHT, TIGHT if k == 0 else self.halo.shape[2] - TIGHT)
+
+    def start(self, sources, k):
+        self.copies[k] = [
+            send(sources[g].at[self.rows(k)], self.halo.at[g, self.n, self.rows(k)], self.pair(k, g), self.peers[g])
             for g in range(3)
         ]
 
-    def finish(self):
-        across = []
-        for g in (0, 2):
-            self.copies[g].wait()
-            got = self.halo.at[g, self.n]
-            across.append(send(got, got, (self.sems.at[0, 3 + g], self.sems.at[1, 3 + g]), self.partner))
-        self.copies[1].wait()
-        for copy in across:
+    def forward(self):
+        self.across = []
+        for k in range(B):
+            for g in (0, 2):
+                self.copies[k][g].wait()
+                got = self.halo.at[g, self.n, self.rows(k)]
+                self.across.append(send(got, got, self.pair(k, 3 + g), self.partner))
+
+    def settle(self):
+        for k in range(B):
+            self.copies[k][1].wait()
+        for copy in self.across:
             copy.wait()
 
 
@@ -277,23 +309,21 @@
             copy.wait()
         for t in range(B):
             for g in range(3):
-                faces = self.arrived[g, t * FACES : (t + 1) * FACES].astype(F32)
+                faces = stretch(self.arrived[g, t * TIGHT_FACES : (t + 1) * TIGHT_FACES].astype(F32))
                 add_faces(faces.reshape(FACES // 8, 8, L), grads, t)
 
 
 class Sum:
-    def __init__(self, nz, nxy, src, whole, scratch):
-        self.nz, self.nxy, self.src, self.whole = nz, nxy, src, whole
-        (self.half, self.sums, self.fixed, self.got1, self.got2, self.got3,
-         self.sem1, self.sem2, self.sem3, self.sem4, self.sem5, self.sem6) = scratch
+    def __init__(self, nz, nxy, src, whole, at, scratch):
+        self.nz, self.nxy, self.src, self.whole, self.at = nz, nxy, src, whole, at
+        (self.half, self.got1, self.got2, self.got3,
+         self.sem1, self.sem2, self.sem3, self.sem4, self.sem5) = scratch
         w, self.n = lax.axis_index("wide"), lax.axis_index("narrow")
         self.z, self.xy = w // nxy, lax.rem(w, nxy)
-        self.plane = ROWS // nxy
-        self.piece = self.plane // nz
+        self.plane = HALF // nxy
         self.partner = (w, 1 - self.n)
         self.in_plane = [(self.z * nxy + lax.rem(self.xy + d, nxy), self.n) for d in range(1, nxy)]
         self.in_column = [(lax.rem(self.z + d, nz) * nxy + self.xy, self.n) for d in range(1, nz)]
-        self.crossing = []
 
     def peers(self):
         return [self.partner] + self.in_plane + self.in_column
@@ -304,65 +334,50 @@
     def pair(self, sems, d):
         return sems.at[0, d], sems.at[1, d]
 
-    def cores(self, i):
-        theirs = self.src.at[self.rows(i * ROWS + (1 - self.n) * HALF, HALF)]
-        self.crossing.append(send(theirs, self.got1.at[i], self.pair(self.sem1, i), self.partner))
+    def cores(self):
+        theirs = self.src.at[self.rows((1 - self.n) * HALF, HALF)]
+        self.copies = [send(theirs, self.got1, self.pair(self.sem1, 0), self.partner)]
 
     def wait(self):
         for copy in self.copies:
             copy.wait()
 
     def planes(self):
-        for i, copy in enumerate(self.crossing):
-            copy.wait()
-            mine = self.src[self.rows(i * ROWS + self.n * HALF, HALF), :]
-            self.half[i * HALF : (i + 1) * HALF] = (mine + self.got1[i]).astype(BF16)
+        self.wait()
+        mine = self.src[self.rows(self.n * HALF, HALF), :]
+        self.half[...] = (mine + self.got1[...]).astype(BF16)
         self.copies = []
         for d, peer in enumerate(self.in_plane):
             to = lax.rem(self.xy + d + 1, self.nxy)
             part = self.half.at[self.rows(to * self.plane, self.plane)]
             self.copies.append(send(part, self.got2.at[d], self.pair(self.sem2, d), peer))
 
-    def columns(self):
+    def column(self):
         self.wait()
         total = self.half[self.rows(self.xy * self.plane, self.plane), :].astype(F32)
         for d in range(self.nxy - 1):
             total += self.got2[d].astype(F32)
-        self.sums[...] = total
-        self.copies = []
-        for d, peer in enumerate(self.in_column):
-            to = lax.rem(self.z + d + 1, self.nz)
-            part = self.sums.at[self.rows(to * self.piece, self.piece)]
-            self.copies.append(send(part, self.got3.at[d], self.pair(self.sem3, d), peer))
-
-    def columns_back(self):
-        self.wait()
-        own = self.rows(self.z * self.piece, self.piece)
-        total = self.sums[own, :]
-        for d in range(self.nz - 1):
-            total += self.got3[d]
-        self.fixed[own, :] = total
-        self.copies = [
-            send(self.fixed.at[own], self.fixed.at[own], self.pair(self.sem4, d), peer)
-            for d, peer in enumerate(self.in_column)
-        ]
+        own = self.got3.at[self.z]
+        own[...] = total.astype(BF16)
+        self.copies = [send(own, own, self.pair(self.sem3, d), peer) for d, peer in enumerate(self.in_column)]
 
     def planes_back(self):
         self.wait()
-        own = self.rows(self.n * ROWS + self.xy * self.plane, self.plane)
-        self.whole[own, :] = self.fixed[...].astype(BF16)
-        self.copies = [
-            send(self.whole.at[own], self.whole.at[own], self.pair(self.sem5, d), peer)
-            for d, peer in enumerate(self.in_plane)
-        ]
-        self.across = [send(self.whole.at[own], self.whole.at[own], self.pair(self.sem6, self.nxy - 1), self.partner)]
+        total = self.got3[0].astype(F32)
+        for z in range(1, self.nz):
+            total += self.got3[z].astype(F32)
+        own = self.rows(self.at + self.n * HALF + self.xy * self.plane, self.plane)
+        self.whole[own, :] = total.astype(BF16)
+        own = self.whole.at[own]
+        self.copies = [send(own, own, self.pair(self.sem4, d), peer) for d, peer in enumerate(self.in_plane)]
+        self.across = [send(own, own, self.pair(self.sem5, self.nxy - 1), self.partner)]
 
     def cores_back(self):
         for d, copy in enumerate(self.copies):
             copy.wait()
             origin = lax.rem(self.xy + self.nxy - d - 1, self.nxy)
-            got = self.rows(self.n * ROWS + origin * self.plane, self.plane)
-            self.across.append(send(self.whole.at[got], self.whole.at[got], self.pair(self.sem6, d), self.partner))
+            got = self.whole.at[self.rows(self.at + self.n * HALF + origin * self.plane, self.plane)]
+            self.across.append(send(got, got, self.pair(self.sem5, d), self.partner))
 
     def end(self):
         for copy in self.across:
@@ -370,49 +385,54 @@
 
 
 def sum_scratch(nz, nxy):
-    plane = ROWS // nxy
-    sems = [pltpu.SemaphoreType.DMA((2, count)) for count in (2, nxy - 1, nz - 1, nz - 1, nxy - 1, nxy)]
+    plane = HALF // nxy
+    sems = [pltpu.SemaphoreType.DMA((2, count)) for count in (1, nxy - 1, nz - 1, nxy - 1, nxy)]
     return [
-        pltpu.VMEM((ROWS, L), BF16),
-        pltpu.VMEM((plane, L), F32),
-        pltpu.VMEM((plane, L), F32),
-        pltpu.VMEM((2, HALF, L), F32),
+        pltpu.VMEM((HALF, L), BF16),
+        pltpu.VMEM((HALF, L), F32),
         pltpu.VMEM((nxy - 1, plane, L), BF16),
-        pltpu.VMEM((nz - 1, plane // nz, L), F32),
+        pltpu.VMEM((nz, plane, L), BF16),
     ] + sems
 
 
-def main_kernel(nz, nxy, slots, plan, features, occupancy, out_grad, weights1, weights2,
+def main_kernel(nz, nxy, slots, plan, features, occupancy, out_grad, far_weights1, far_weights2,
                 output, feature_grad, reduced,
                 table, shifted, columns, side, back, around, padded, middle, low, high, planes, edges, faces, grads,
-                mask, slope, chosen, shell, masked, pre, sums, packed, whole,
+                mask, slope, chosen, shell, masked, pre, sums, packed1, packed2, weights1, weights2,
                 messages, near, hidden_shells, hidden_near,
                 out1, got1, joined1, arrived1, out2, got2, joined2, arrived2,
-                near_sems, hidden_sems, back_sems1, back_sems2, *scratch):
+                near_sems, hidden_sems, back_sems1, back_sems2, load_sems, *scratch):
     n_wide = nz * nxy
     n = lax.axis_index("narrow")
     actives = Shells(n_wide, near, near_sems)
     hiddens = Shells(n_wide, hidden_near, hidden_sems)
     returns1 = Returns(n_wide, out1, got1, joined1, arrived1, back_sems1)
     returns2 = Returns(n_wide, out2, got2, joined2, arrived2, back_sems2)
-    total = Sum(nz, nxy, packed, whole, scratch)
-    everyone = [actives.peers[0], actives.peers[2]] + total.peers()
+    total1 = Sum(nz, nxy, packed1, reduced, 0, scratch[: len(scratch) // 2])
+    total2 = Sum(nz, nxy, packed2, reduced, ROWS, scratch[len(scratch) // 2 :])
+    everyone = [actives.peers[0], actives.peers[2]] + total1.peers()
     greet(everyone)
+    load1 = pltpu.make_async_copy(far_weights1, weights1, load_sems.at[0])
+    load2 = pltpu.make_async_copy(far_weights2, weights2, load_sems.at[1])
+    load2.start()
+    load1.start()
 
     for t in range(B):
         seen = occupancy[t : t + 1, :].astype(F32)
         table[t] = to_rows(features[t].astype(F32) * seen).reshape(8, 8, 8, L)
     row = lax.broadcasted_iota(jnp.int32, (16, L), 0)
-    pack_own(table, shell, messages.at[0])
+    for t in range(B):
+        pack_own(table, shell, messages.at[0], t)
     for g in range(3):
         if g > 0:
-            messages[g, 0 : 2 * SHELL] = messages[0, 0 : 2 * SHELL]
+            messages[g, 0 : 2 * TIGHT] = messages[0, 0 : 2 * TIGHT]
         rows = jnp.zeros((16, L), F32)
         for i in range(4):
-            rows = jnp.where(row == i, plan[0, g, i // 2, i % 2].astype(F32), rows)
-        messages[g, 2 * SHELL : MESSAGE] = rows.astype(BF16)
+            rows = jnp.where(row == i, plan[i, g].astype(F32), rows)
+        messages[g, 2 * TIGHT : MESSAGE] = rows.astype(BF16)
     pl.semaphore_wait(pltpu.get_barrier_semaphore(), len(everyone))
-    actives.start([messages.at[g] for g in range(3)])
+    for t in range(B):
+        actives.start([messages.at[g] for g in range(3)], t)
 
     padded[...] = jnp.zeros_like(padded)
     masked[C:L] = jnp.zeros((L - C, B * V), BF16)
@@ -437,12 +457,15 @@
         for t in range(B):
             add_faces(faces[t], grads, t)
 
+    load2.wait()
     transpose(weights2)
+    load1.wait()
     side_weights(weights1, side)
     table[EMPTY] = jnp.zeros((8, 8, 8, L), F32)
-    actives.finish()
+    actives.forward()
+    actives.settle()
     for source in range(SLOTS // 2):
-        rows = near[source // 2, source % 2, 2 * SHELL : MESSAGE].astype(F32)
+        rows = near[source // 2, source % 2, 2 * TIGHT : MESSAGE].astype(F32)
         for c in range(2):
             row = jnp.where(n == 0, rows[c : c + 1], rows[2 + c : 3 + c])
             chosen[2 * source + c] = jnp.broadcast_to(row, (8, L))
@@ -459,9 +482,9 @@
         seen = mask[t]
         gate = jax.nn.sigmoid(value)
         table[t] = (value * gate * seen).astype(BF16).astype(F32).reshape(8, 8, 8, L)
+        pack_own(table, shell, hidden_shells, t)
+        hiddens.start([hidden_shells] * 3, t)
         slope[t] = seen * gate * (1.0 + value * (1.0 - gate))
-    pack_own(table, shell, hidden_shells)
-    hiddens.start([hidden_shells] * 3)
     side_weights(weights2, side)
     returns1.add(grads)
     for t in range(B):
@@ -469,20 +492,24 @@
         padded[t, 2:10, 2:10] = grad.reshape(8, 8, 8, L)
         pre[:, t * V : (t + 1) * V] = grad.T.astype(BF16)
     weight_sums(pre, columns, sums)
-    pack_sums(sums, packed, 0)
-    total.cores(0)
-
-    hiddens.finish()
+    pack_sums(sums, packed1, 0)
+    total1.cores()
+
+    hiddens.forward()
+    total1.planes()
+    hiddens.settle()
     halo_entries(table, hidden_near, chosen)
     build_columns(slots, table, shifted, columns)
     weight_sums(masked, columns, sums)
-    pack_sums(sums, packed, ROWS)
-    total.cores(1)
-    total.planes()
+    pack_sums(sums, packed2, 0)
+    total2.cores()
+    total1.column()
+    total2.planes()
     transpose(weights1)
     gather_gradients(faces, chosen, out2)
     returns2.start()
-    total.columns()
+    total2.column()
+    total1.planes_back()
     returns2.join()
 
     def forward(t):
@@ -493,37 +520,26 @@
         output[t] = ((features[t].astype(F32) * seen + value[0:C]) * seen).astype(BF16)
 
     forward(0)
-    total.columns_back()
     forward(1)
-    total.planes_back()
+    total1.cores_back()
+    total2.planes_back()
     returns2.add(grads)
     for t in range(B):
         seen = occupancy[t : t + 1, :].astype(F32)
         own = grads[t].reshape(V, L).T
         feature_grad[t] = ((out_grad[t].astype(F32) * seen + own[0:C]) * seen).astype(BF16)
-    total.cores_back()
-    total.end()
-    reduced[...] = whole[...]
+    total1.end()
+    total2.cores_back()
+    total2.end()
 
 
 VMEM_SPEC = pl.BlockSpec(memory_space=pltpu.VMEM)
 SMEM_SPEC = pl.BlockSpec(memory_space=pltpu.SMEM)
+ANY_SPEC = pl.BlockSpec(memory_space=pl.ANY)
 
 
 def shape(dims, dtype):
     return jax.ShapeDtypeStruct(dims, dtype)
-
-
-def local_call(body, outs, scratch, scalars, *args):
-    specs = [SMEM_SPEC] * scalars + [VMEM_SPEC] * (len(args) - scalars)
-    return pl.pallas_call(
-        body,
-        out_shape=outs,
-        in_specs=specs,
-        out_specs=[VMEM_SPEC] * len(outs),
-        scratch_shapes=[pltpu.VMEM(dims, dtype) for dims, dtype in scratch],
-        compiler_params=pltpu.CompilerParams(vmem_limit_bytes=VMEM_LIMIT),
-    )(*args)
 
 
 BLOCK = (8, 8, 8, L)
@@ -549,17 +565,19 @@
     ((L, B * V), BF16),
     ((L, B * V), BF16),
     ((WG, L), F32),
-    ((2 * ROWS, L), F32),
-    ((2 * ROWS, L), BF16),
+    ((ROWS, L), F32),
+    ((ROWS, L), F32),
+    ((27, C, C), BF16),
+    ((27, C, C), BF16),
     ((3, MESSAGE, L), BF16),
     ((3, 2, MESSAGE, L), BF16),
-    ((2 * SHELL, L), BF16),
-    ((3, 2, 2 * SHELL, L), BF16),
+    ((2 * TIGHT, L), BF16),
+    ((3, 2, 2 * TIGHT, L), BF16),
 ] + 2 * [
-    ((3, 2, 2 * FACES, L), BF16),
-    ((2, 2 * FACES, L), BF16),
-    ((2, 2 * FACES, L), BF16),
-    ((3, 2 * FACES, L), BF16),
+    ((3, 2, 2 * TIGHT_FACES, L), BF16),
+    ((2, 2 * TIGHT_FACES, L), BF16),
+    ((2, 2 * TIGHT_FACES, L), BF16),
+    ((3, 2 * TIGHT_FACES, L), BF16),
 ]
 
 
@@ -569,14 +587,14 @@
     output, feature_grad, reduced = pl.pallas_call(
         functools.partial(main_kernel, nz, nxy),
         out_shape=[blocks, blocks, shape((2 * ROWS, L), BF16)],
-        in_specs=[SMEM_SPEC] * 2 + [VMEM_SPEC] * 5,
+        in_specs=[SMEM_SPEC] * 2 + [VMEM_SPEC] * 3 + [ANY_SPEC] * 2,
         out_specs=[VMEM_SPEC] * 3,
         scratch_shapes=[pltpu.VMEM(dims, dtype) for dims, dtype in SCRATCH]
-        + [dma((2, 6)), dma((2, 6)), dma((2, 5)), dma((2, 5))] + sum_scratch(nz, nxy),
+        + [dma((2, 2, 6)), dma((2, 2, 6)), dma((2, 5)), dma((2, 5)), dma((2,))] + 2 * sum_scratch(nz, nxy),
         compiler_params=pltpu.CompilerParams(
             collective_id=0, has_side_effects=True, vmem_limit_bytes=VMEM_LIMIT
         ),
-    )(slots, send_blocks, features, occupancy, out_grad, conv1_weight, conv2_weight)
+    )(slots, send_blocks.reshape(3, 4).T, features, occupancy, out_grad, conv1_weight, conv2_weight)
     scale = (B * V * 2 * nz * nxy) ** -0.5
     return pl.pallas_call(
         functools.partial(last_kernel, scale),

time: 77.5 us -> 68.3 us (0.88)
  Pallas kernels: 75.3 us -> 67.6 us
  local copies, waits for them, and re-layouts: 1.34 us -> 0 us
    pallas_call x1, Pallas kernels: 71.8 us -> 64.1 us  [local(): pl.pallas_call(functools.partial(main_kernel, nz, nxy), out_shape=[blocks...]
    unnamed x1 -> x0, local copies, waits for them, and re-layouts: 1.34 us -> none
where the time goes in v4:
time: 68.3 us; the launch traced here: 68.2 us
  Pallas kernels  67.6 us (99%)
    pallas_call x1, Pallas kernels, local(): pl.pallas_call(functools.partial(main_kernel, nz, nxy), out_shape=[blocks...  64.1 us
    pallas_call x1, Pallas kernels, local(): pl.pallas_call(functools.partial(last_kernel, scale), out_shape=[blocks,...  3.5 us

profile of v4, /device:TPU:1, one launch (start us, length us, event | category | flops | bytes accessed | tf_op | source)
XLA Modules:
  0.0 68.2 jit_solution(10661382875564061408)
XLA Ops:
  0.6 64.1 %shard_map.102 = (bf16[2,96,512]{2,1,0:T(8,128)(2,1)}, bf16[2,96,512]{2,1,0:T(8,128)(2,1)}, bf16[4096,128]{1,0:T(8,128)(2,1)}) custom-call(s32[2,27]{1,0:T(2,128)} %slots.1, s32[4,3]{1,0:T(4,128)} %bitcast.3, bf16[2,96,512]{2,1,0:T(8,128)(2,1)} %features.1, s32[2,512]{1,0:T(2,128)} %occupancy.1, bf16[2,96,512]{2,1,0:T(8,128)(2,1)} %out_grad.1, ...), custom_call_target="tpu_custom_call" | custom-call | tf_op jit(solution)/shard_map/pallas_call | solution.py:587
  64.7 3.5 %shard_map.103 = (bf16[2,96,512]{2,1,0:T(8,128)(2,1)}, bf16[2,96,512]{2,1,0:T(8,128)(2,1)}, f32[27,96,96]{2,1,0:T(8,128)}, f32[27,96,96]{2,1,0:T(8,128)}) custom-call(bf16[4096,128]{1,0:T(8,128)(2,1)} %get-tuple-element.7.packed, bf16[2,96,512]{2,1,0:T(8,128)(2,1)} %get-tuple-element.8.output, bf16[2,96,512]{2,1,0:T(8,128)(2,1)} %get-tuple-element.9.grad), custom_call_target="tpu_custom_call" | custom-call | tf_op jit(solution)/shard_map/pallas_call | solution.py:599

commit v5 on v4

--- a/solution.py
+++ b/solution.py
@@ -322,8 +322,23 @@
         self.z, self.xy = w // nxy, lax.rem(w, nxy)
         self.plane = HALF // nxy
         self.partner = (w, 1 - self.n)
-        self.in_plane = [(self.z * nxy + lax.rem(self.xy + d, nxy), self.n) for d in range(1, nxy)]
-        self.in_column = [(lax.rem(self.z + d, nz) * nxy + self.xy, self.n) for d in range(1, nz)]
+        nx = 4 if nxy % 4 == 0 else nxy
+        ny = nxy // nx
+        x, y = lax.rem(self.xy, nx), self.xy // nx
+
+        def place(dx, dy):
+            return lax.rem(y + dy + ny, ny) * nx + lax.rem(x + dx + nx, nx)
+
+        def hops(step, size):
+            return min(step, size - step)
+
+        steps = [(dx, dy) for dx in range(nx) for dy in range(ny) if dx or dy]
+        steps.sort(key=lambda step: -hops(step[0], nx) - hops(step[1], ny))
+        self.to = [place(dx, dy) for dx, dy in steps]
+        self.origin = [place(-dx, -dy) for dx, dy in steps]
+        self.in_plane = [(self.z * nxy + to, self.n) for to in self.to]
+        rises = sorted(range(1, nz), key=lambda rise: -hops(rise, nz))
+        self.in_column = [(lax.rem(self.z + rise, nz) * nxy + self.xy, self.n) for rise in rises]
 
     def peers(self):
         return [self.partner] + self.in_plane + self.in_column
@@ -348,8 +363,7 @@
         self.half[...] = (mine + self.got1[...]).astype(BF16)
         self.copies = []
         for d, peer in enumerate(self.in_plane):
-            to = lax.rem(self.xy + d + 1, self.nxy)
-            part = self.half.at[self.rows(to * self.plane, self.plane)]
+            part = self.half.at[self.rows(self.to[d] * self.plane, self.plane)]
             self.copies.append(send(part, self.got2.at[d], self.pair(self.sem2, d), peer))
 
     def column(self):
@@ -375,8 +389,7 @@
     def cores_back(self):
         for d, copy in enumerate(self.copies):
             copy.wait()
-            origin = lax.rem(self.xy + self.nxy - d - 1, self.nxy)
-            got = self.whole.at[self.rows(self.at + self.n * HALF + origin * self.plane, self.plane)]
+            got = self.whole.at[self.rows(self.at + self.n * HALF + self.origin[d] * self.plane, self.plane)]
             self.across.append(send(got, got, self.pair(self.sem5, d), self.partner))
 
     def end(self):
@@ -395,10 +408,10 @@
     ] + sems
 
 
-def main_kernel(nz, nxy, slots, plan, features, occupancy, out_grad, far_weights1, far_weights2,
+def main_kernel(nz, nxy, slots, plan, far_features, far_occupancy, far_out_grad, far_weights1, far_weights2,
                 output, feature_grad, reduced,
                 table, shifted, columns, side, back, around, padded, middle, low, high, planes, edges, faces, grads,
-                mask, slope, chosen, shell, masked, pre, sums, packed1, packed2, weights1, weights2,
+                mask, slope, chosen, shell, masked, pre, sums, packed1, packed2, features, occupancy, out_grad, weights1, weights2,
                 messages, near, hidden_shells, hidden_near,
                 out1, got1, joined1, arrived1, out2, got2, joined2, arrived2,
                 near_sems, hidden_sems, back_sems1, back_sems2, load_sems, *scratch):
@@ -412,10 +425,13 @@
     total2 = Sum(nz, nxy, packed2, reduced, ROWS, scratch[len(scratch) // 2 :])
     everyone = [actives.peers[0], actives.peers[2]] + total1.peers()
     greet(everyone)
-    load1 = pltpu.make_async_copy(far_weights1, weights1, load_sems.at[0])
-    load2 = pltpu.make_async_copy(far_weights2, weights2, load_sems.at[1])
-    load2.start()
-    load1.start()
+    far = (far_occupancy, far_features, far_out_grad, far_weights2, far_weights1)
+    loads = []
+    for i, (source, dest) in enumerate(zip(far, (occupancy, features, out_grad, weights2, weights1))):
+        loads.append(pltpu.make_async_copy(source, dest, load_sems.at[i]))
+        loads[i].start()
+    loads[0].wait()
+    loads[1].wait()
 
     for t in range(B):
         seen = occupancy[t : t + 1, :].astype(F32)
@@ -434,6 +450,7 @@
     for t in range(B):
         actives.start([messages.at[g] for g in range(3)], t)
 
+    loads[2].wait()
     padded[...] = jnp.zeros_like(padded)
     masked[C:L] = jnp.zeros((L - C, B * V), BF16)
     for t in range(B):
@@ -457,9 +474,9 @@
         for t in range(B):
             add_faces(faces[t], grads, t)
 
-    load2.wait()
+    loads[3].wait()
     transpose(weights2)
-    load1.wait()
+    loads[4].wait()
     side_weights(weights1, side)
     table[EMPTY] = jnp.zeros((8, 8, 8, L), F32)
     actives.forward()
@@ -503,14 +520,6 @@
     weight_sums(masked, columns, sums)
     pack_sums(sums, packed2, 0)
     total2.cores()
-    total1.column()
-    total2.planes()
-    transpose(weights1)
-    gather_gradients(faces, chosen, out2)
-    returns2.start()
-    total2.column()
-    total1.planes_back()
-    returns2.join()
 
     def forward(t):
         seen = occupancy[t : t + 1, :].astype(F32)
@@ -520,16 +529,24 @@
         output[t] = ((features[t].astype(F32) * seen + value[0:C]) * seen).astype(BF16)
 
     forward(0)
+    total2.planes()
+    total1.column()
+    transpose(weights1)
+    gather_gradients(faces, chosen, out2)
+    returns2.start()
+    total2.column()
+    returns2.join()
     forward(1)
-    total1.cores_back()
+    total1.planes_back()
     total2.planes_back()
     returns2.add(grads)
     for t in range(B):
         seen = occupancy[t : t + 1, :].astype(F32)
         own = grads[t].reshape(V, L).T
         feature_grad[t] = ((out_grad[t].astype(F32) * seen + own[0:C]) * seen).astype(BF16)
+    total1.cores_back()
+    total2.cores_back()
     total1.end()
-    total2.cores_back()
     total2.end()
 
 
@@ -567,6 +584,9 @@
     ((WG, L), F32),
     ((ROWS, L), F32),
     ((ROWS, L), F32),
+    ((B, C, V), BF16),
+    ((B, V), jnp.int32),
+    ((B, C, V), BF16),
     ((27, C, C), BF16),
     ((27, C, C), BF16),
     ((3, MESSAGE, L), BF16),
@@ -587,10 +607,10 @@
     output, feature_grad, reduced = pl.pallas_call(
         functools.partial(main_kernel, nz, nxy),
         out_shape=[blocks, blocks, shape((2 * ROWS, L), BF16)],
-        in_specs=[SMEM_SPEC] * 2 + [VMEM_SPEC] * 3 + [ANY_SPEC] * 2,
+        in_specs=[SMEM_SPEC] * 2 + [ANY_SPEC] * 5,
         out_specs=[VMEM_SPEC] * 3,
         scratch_shapes=[pltpu.VMEM(dims, dtype) for dims, dtype in SCRATCH]
-        + [dma((2, 2, 6)), dma((2, 2, 6)), dma((2, 5)), dma((2, 5)), dma((2,))] + 2 * sum_scratch(nz, nxy),
+        + [dma((2, 2, 6)), dma((2, 2, 6)), dma((2, 5)), dma((2, 5)), dma((5,))] + 2 * sum_scratch(nz, nxy),
         compiler_params=pltpu.CompilerParams(
             collective_id=0, has_side_effects=True, vmem_limit_bytes=VMEM_LIMIT
         ),

time: 68.3 us -> 67 us (0.981)
  Pallas kernels: 67.6 us -> 66.2 us
    pallas_call x1, Pallas kernels: 64.1 us -> 62.7 us  [local(): pl.pallas_call(functools.partial(main_kernel, nz, nxy), out_shape=[blocks...]
where the time goes in v5:
time: 67 us; the launch traced here: 66.9 us
  Pallas kernels  66.2 us (99%)
    pallas_call x1, Pallas kernels, local(): pl.pallas_call(functools.partial(main_kernel, nz, nxy), out_shape=[blocks...  62.7 us
    pallas_call x1, Pallas kernels, local(): pl.pallas_call(functools.partial(last_kernel, scale), out_shape=[blocks,...  3.5 us

profile of v5, /device:TPU:1, one launch (start us, length us, event | category | flops | bytes accessed | tf_op | source)
XLA Modules:
  0.0 66.9 jit_solution(14559207678149293724)
XLA Ops:
  0.6 62.7 %shard_map.102 = (bf16[2,96,512]{2,1,0:T(8,128)(2,1)}, bf16[2,96,512]{2,1,0:T(8,128)(2,1)}, bf16[4096,128]{1,0:T(8,128)(2,1)}) custom-call(s32[2,27]{1,0:T(2,128)} %slots.1, s32[4,3]{1,0:T(4,128)} %bitcast.3, bf16[2,96,512]{2,1,0:T(8,128)(2,1)} %far_features.1, s32[2,512]{1,0:T(2,128)} %far_occupancy.1, bf16[2,96,512]{2,1,0:T(8,128)(2,1)} %far_out_grad.1, ...), custom_call_target="tpu_custom_call" | custom-call | tf_op jit(solution)/shard_map/pallas_call | solution.py:607
  63.4 3.5 %shard_map.103 = (bf16[2,96,512]{2,1,0:T(8,128)(2,1)}, bf16[2,96,512]{2,1,0:T(8,128)(2,1)}, f32[27,96,96]{2,1,0:T(8,128)}, f32[27,96,96]{2,1,0:T(8,128)}) custom-call(bf16[4096,128]{1,0:T(8,128)(2,1)} %get-tuple-element.7.packed, bf16[2,96,512]{2,1,0:T(8,128)(2,1)} %get-tuple-element.8.output, bf16[2,96,512]{2,1,0:T(8,128)(2,1)} %get-tuple-element.9.grad), custom_call_target="tpu_custom_call" | custom-call | tf_op jit(solution)/shard_map/pallas_call | solution.py:619

commit v6 on v5

--- a/solution.py
+++ b/solution.py
@@ -29,7 +29,8 @@
 MESSAGE = 2 * TIGHT + 16
 FACES = 384
 TIGHT_FACES = FACES * 3 // 4
-VMEM_LIMIT = 56 * 1024 * 1024
+VMEM_LIMIT = 44 * 1024 * 1024
+LAST_LIMIT = 12 * 1024 * 1024
 
 
 def direction(a, b, e):
@@ -341,7 +342,7 @@
         self.in_column = [(lax.rem(self.z + rise, nz) * nxy + self.xy, self.n) for rise in rises]
 
     def peers(self):
-        return [self.partner] + self.in_plane + self.in_column
+        return self.in_column + self.in_plane + [self.partner]
 
     def rows(self, at, size):
         return pl.ds(pl.multiple_of(at, size), size)
@@ -408,13 +409,13 @@
     ] + sems
 
 
-def main_kernel(nz, nxy, slots, plan, far_features, far_occupancy, far_out_grad, far_weights1, far_weights2,
+def main_kernel(nz, nxy, far_slots, far_plan, far_features, far_occupancy, far_out_grad, far_weights1, far_weights2,
                 output, feature_grad, reduced,
                 table, shifted, columns, side, back, around, padded, middle, low, high, planes, edges, faces, grads,
                 mask, slope, chosen, shell, masked, pre, sums, packed1, packed2, features, occupancy, out_grad, weights1, weights2,
                 messages, near, hidden_shells, hidden_near,
                 out1, got1, joined1, arrived1, out2, got2, joined2, arrived2,
-                near_sems, hidden_sems, back_sems1, back_sems2, load_sems, *scratch):
+                near_sems, hidden_sems, back_sems1, back_sems2, load_sems, slots, plan, *scratch):
     n_wide = nz * nxy
     n = lax.axis_index("narrow")
     actives = Shells(n_wide, near, near_sems)
@@ -423,11 +424,11 @@
     returns2 = Returns(n_wide, out2, got2, joined2, arrived2, back_sems2)
     total1 = Sum(nz, nxy, packed1, reduced, 0, scratch[: len(scratch) // 2])
     total2 = Sum(nz, nxy, packed2, reduced, ROWS, scratch[len(scratch) // 2 :])
-    everyone = [actives.peers[0], actives.peers[2]] + total1.peers()
+    everyone = total1.peers() + [actives.peers[0], actives.peers[2]]
     greet(everyone)
-    far = (far_occupancy, far_features, far_out_grad, far_weights2, far_weights1)
+    far = (far_occupancy, far_features, far_plan, far_out_grad, far_weights2, far_slots, far_weights1)
     loads = []
-    for i, (source, dest) in enumerate(zip(far, (occupancy, features, out_grad, weights2, weights1))):
+    for i, (source, dest) in enumerate(zip(far, (occupancy, features, plan, out_grad, weights2, slots, weights1))):
         loads.append(pltpu.make_async_copy(source, dest, load_sems.at[i]))
         loads[i].start()
     loads[0].wait()
@@ -437,6 +438,7 @@
         seen = occupancy[t : t + 1, :].astype(F32)
         table[t] = to_rows(features[t].astype(F32) * seen).reshape(8, 8, 8, L)
     row = lax.broadcasted_iota(jnp.int32, (16, L), 0)
+    loads[2].wait()
     for t in range(B):
         pack_own(table, shell, messages.at[0], t)
     for g in range(3):
@@ -450,7 +452,7 @@
     for t in range(B):
         actives.start([messages.at[g] for g in range(3)], t)
 
-    loads[2].wait()
+    loads[3].wait()
     padded[...] = jnp.zeros_like(padded)
     masked[C:L] = jnp.zeros((L - C, B * V), BF16)
     for t in range(B):
@@ -474,9 +476,10 @@
         for t in range(B):
             add_faces(faces[t], grads, t)
 
-    loads[3].wait()
+    loads[4].wait()
+    loads[5].wait()
     transpose(weights2)
-    loads[4].wait()
+    loads[6].wait()
     side_weights(weights1, side)
     table[EMPTY] = jnp.zeros((8, 8, 8, L), F32)
     actives.forward()
@@ -490,8 +493,8 @@
     returns1.start()
 
     halo_entries(table, near, chosen)
+    build_columns(slots, table, shifted, columns)
     returns1.join()
-    build_columns(slots, table, shifted, columns)
     for t in range(B):
         value = lax.dot_general(
             columns[t * V : (t + 1) * V, :], side[...], (((1,), (1,)), ((), ())), preferred_element_type=F32
@@ -551,8 +554,7 @@
 
 
 VMEM_SPEC = pl.BlockSpec(memory_space=pltpu.VMEM)
-SMEM_SPEC = pl.BlockSpec(memory_space=pltpu.SMEM)
-ANY_SPEC = pl.BlockSpec(memory_space=pl.ANY)
+HBM_SPEC = pl.BlockSpec(memory_space=pltpu.HBM)
 
 
 def shape(dims, dtype):
@@ -604,24 +606,25 @@
 def local(nz, nxy, features, occupancy, conv1_weight, conv2_weight, out_grad, slots, send_blocks):
     dma = pltpu.SemaphoreType.DMA
     blocks = shape((B, C, V), BF16)
+    inputs = (slots, send_blocks.reshape(3, 4).T, features, occupancy, out_grad, conv1_weight, conv2_weight)
     output, feature_grad, reduced = pl.pallas_call(
         functools.partial(main_kernel, nz, nxy),
         out_shape=[blocks, blocks, shape((2 * ROWS, L), BF16)],
-        in_specs=[SMEM_SPEC] * 2 + [ANY_SPEC] * 5,
+        in_specs=[HBM_SPEC] * 7,
         out_specs=[VMEM_SPEC] * 3,
         scratch_shapes=[pltpu.VMEM(dims, dtype) for dims, dtype in SCRATCH]
-        + [dma((2, 2, 6)), dma((2, 2, 6)), dma((2, 5)), dma((2, 5)), dma((5,))] + 2 * sum_scratch(nz, nxy),
+        + [dma((2, 2, 6)), dma((2, 2, 6)), dma((2, 5)), dma((2, 5)), dma((7,)), pltpu.SMEM((B, 27), jnp.int32), pltpu.SMEM((4, 3), jnp.int32)] + 2 * sum_scratch(nz, nxy),
         compiler_params=pltpu.CompilerParams(
             collective_id=0, has_side_effects=True, vmem_limit_bytes=VMEM_LIMIT
         ),
-    )(slots, send_blocks.reshape(3, 4).T, features, occupancy, out_grad, conv1_weight, conv2_weight)
+    )(*(pltpu.with_memory_space_constraint(x, pltpu.HBM) for x in inputs))
     scale = (B * V * 2 * nz * nxy) ** -0.5
     return pl.pallas_call(
         functools.partial(last_kernel, scale),
         out_shape=[blocks, blocks] + [shape((27, C, C), F32)] * 2,
         in_specs=[VMEM_SPEC] * 3,
         out_specs=[VMEM_SPEC] * 4,
-        compiler_params=pltpu.CompilerParams(vmem_limit_bytes=VMEM_LIMIT),
+        compiler_params=pltpu.CompilerParams(vmem_limit_bytes=LAST_LIMIT),
     )(reduced, output, feature_grad)
 
 

time: 67 us -> 64.7 us (0.966)
  Pallas kernels: 66.2 us -> 63.9 us
    pallas_call x1, Pallas kernels: 3.5 us -> 2.15 us  [local(): pl.pallas_call(functools.partial(last_kernel, scale), out_shape=[blocks,...]
    pallas_call x1, Pallas kernels: 62.7 us -> 61.8 us  [local(): pl.pallas_call(functools.partial(main_kernel, nz, nxy), out_shape=[blocks...]
where the time goes in v6:
time: 64.7 us; the launch traced here: 64.6 us
  Pallas kernels  63.9 us (99%)
    pallas_call x1, Pallas kernels, local(): pl.pallas_call(functools.partial(main_kernel, nz, nxy), out_shape=[blocks...  61.8 us
    pallas_call x1, Pallas kernels, local(): pl.pallas_call(functools.partial(last_kernel, scale), out_shape=[blocks,...  2.15 us

profile of v6, /device:TPU:1, one launch (start us, length us, event | category | flops | bytes accessed | tf_op | source)
XLA Modules:
  0.0 64.6 jit_solution(14274172335237629404)
XLA Ops:
  0.6 61.8 %shard_map.102 = (bf16[2,96,512]{2,1,0:T(8,128)(2,1)S(1)}, bf16[2,96,512]{2,1,0:T(8,128)(2,1)S(1)}, bf16[4096,128]{1,0:T(8,128)(2,1)S(1)}) custom-call(s32[2,27]{1,0:T(2,128)} %far_slots.1, s32[4,3]{1,0:T(4,128)} %bitcast.3, bf16[2,96,512]{2,1,0:T(8,128)(2,1)} %far_features.1, s32[2,512]{1,0:T(2,128)} %far_occupancy.1, bf16[2,96,512]{2,1,0:T(8,128)(2,1)} %far_out_grad.1, ...), custom_call_target="tpu_custom_call" | custom-call | tf_op jit(solution)/shard_map/pallas_call | solution.py:610
  62.4 2.2 %shard_map.103 = (bf16[2,96,512]{2,1,0:T(8,128)(2,1)}, bf16[2,96,512]{2,1,0:T(8,128)(2,1)}, f32[27,96,96]{2,1,0:T(8,128)}, f32[27,96,96]{2,1,0:T(8,128)}) custom-call(bf16[4096,128]{1,0:T(8,128)(2,1)S(1)} %get-tuple-element.7.packed, bf16[2,96,512]{2,1,0:T(8,128)(2,1)S(1)} %get-tuple-element.8.output, bf16[2,96,512]{2,1,0:T(8,128)(2,1)S(1)} %get-tuple-element.9.grad), custom_call_target="tpu_custom_call" | custom-call | tf_op jit(solution)/shard_map/pallas_call | solution.py:622

commit v7 on v6

--- a/solution.py
+++ b/solution.py
@@ -250,36 +250,32 @@
 
 
 class Shells:
-    def __init__(self, n_wide, halo, sems):
+    def __init__(self, n_wide, halo, sems, parts):
         self.w, self.n, ahead, behind = neighbours(n_wide)
         self.partner = (self.w, 1 - self.n)
+        self.parts = [pl.ds(start, size) for start, size in parts]
         self.peers = [(behind, self.n), self.partner, (ahead, self.n)]
-        self.halo, self.sems, self.copies = halo, sems, {}
+        self.halo, self.sems, self.copies, self.across = halo, sems, {}, {}
 
     def pair(self, k, i):
         return self.sems.at[0, k, i], self.sems.at[1, k, i]
 
-    def rows(self, k):
-        return pl.ds(k * TIGHT, TIGHT if k == 0 else self.halo.shape[2] - TIGHT)
-
     def start(self, sources, k):
+        rows = self.parts[k]
         self.copies[k] = [
-            send(sources[g].at[self.rows(k)], self.halo.at[g, self.n, self.rows(k)], self.pair(k, g), self.peers[g])
-            for g in range(3)
+            send(sources[g].at[rows], self.halo.at[g, self.n, rows], self.pair(k, g), self.peers[g]) for g in range(3)
         ]
 
-    def forward(self):
-        self.across = []
-        for k in range(B):
-            for g in (0, 2):
-                self.copies[k][g].wait()
-                got = self.halo.at[g, self.n, self.rows(k)]
-                self.across.append(send(got, got, self.pair(k, 3 + g), self.partner))
-
-    def settle(self):
-        for k in range(B):
-            self.copies[k][1].wait()
-        for copy in self.across:
+    def forward(self, k):
+        self.across[k] = []
+        for g in (0, 2):
+            self.copies[k][g].wait()
+            got = self.halo.at[g, self.n, self.parts[k]]
+            self.across[k].append(send(got, got, self.pair(k, 3 + g), self.partner))
+
+    def settle(self, k):
+        self.copies[k][1].wait()
+        for copy in self.across[k]:
             copy.wait()
 
 
@@ -418,8 +414,9 @@
                 near_sems, hidden_sems, back_sems1, back_sems2, load_sems, slots, plan, *scratch):
     n_wide = nz * nxy
     n = lax.axis_index("narrow")
-    actives = Shells(n_wide, near, near_sems)
-    hiddens = Shells(n_wide, hidden_near, hidden_sems)
+    blocks = [(t * TIGHT, TIGHT) for t in range(B)]
+    actives = Shells(n_wide, near, near_sems, [(B * TIGHT, 16)] + blocks)
+    hiddens = Shells(n_wide, hidden_near, hidden_sems, blocks)
     returns1 = Returns(n_wide, out1, got1, joined1, arrived1, back_sems1)
     returns2 = Returns(n_wide, out2, got2, joined2, arrived2, back_sems2)
     total1 = Sum(nz, nxy, packed1, reduced, 0, scratch[: len(scratch) // 2])
@@ -449,8 +446,8 @@
             rows = jnp.where(row == i, plan[i, g].astype(F32), rows)
         messages[g, 2 * TIGHT : MESSAGE] = rows.astype(BF16)
     pl.semaphore_wait(pltpu.get_barrier_semaphore(), len(everyone))
-    for t in range(B):
-        actives.start([messages.at[g] for g in range(3)], t)
+    for k in range(1 + B):
+        actives.start([messages.at[g] for g in range(3)], k)
 
     loads[3].wait()
     padded[...] = jnp.zeros_like(padded)
@@ -462,28 +459,27 @@
         masked[0:C, t * V : (t + 1) * V] = own.astype(BF16)
         padded[t, 2:10, 2:10] = to_rows(own).reshape(8, 8, 8, L)
 
-    def transpose(weights):
-        back_weights(weights, back)
-        faces[...] = jnp.zeros_like(faces)
-
-        def one(t, carry):
-            spread(t, padded, around, back, middle, low, high, planes, edges)
-            scatter(t, slots, middle, planes, edges, faces)
-            grads[t] = middle[1:9, 1:9]
-            return carry
-
-        lax.fori_loop(0, B, one, 0)
+    def transpose(t):
+        spread(t, padded, around, back, middle, low, high, planes, edges)
+        scatter(t, slots, middle, planes, edges, faces)
+        grads[t] = middle[1:9, 1:9]
+
+    def add_own():
         for t in range(B):
             add_faces(faces[t], grads, t)
 
     loads[4].wait()
     loads[5].wait()
-    transpose(weights2)
+    back_weights(weights2, back)
+    faces[...] = jnp.zeros_like(faces)
+    transpose(0)
+    transpose(1)
+    add_own()
     loads[6].wait()
     side_weights(weights1, side)
     table[EMPTY] = jnp.zeros((8, 8, 8, L), F32)
-    actives.forward()
-    actives.settle()
+    actives.forward(0)
+    actives.settle(0)
     for source in range(SLOTS // 2):
         rows = near[source // 2, source % 2, 2 * TIGHT : MESSAGE].astype(F32)
         for c in range(2):
@@ -492,9 +488,13 @@
     gather_gradients(faces, chosen, out1)
     returns1.start()
 
+    for k in (1, 2):
+        actives.forward(k)
+    returns1.join()
+    for k in (1, 2):
+        actives.settle(k)
     halo_entries(table, near, chosen)
     build_columns(slots, table, shifted, columns)
-    returns1.join()
     for t in range(B):
         value = lax.dot_general(
             columns[t * V : (t + 1) * V, :], side[...], (((1,), (1,)), ((), ())), preferred_element_type=F32
@@ -515,9 +515,11 @@
     pack_sums(sums, packed1, 0)
     total1.cores()
 
-    hiddens.forward()
+    for t in range(B):
+        hiddens.forward(t)
     total1.planes()
-    hiddens.settle()
+    for t in range(B):
+        hiddens.settle(t)
     halo_entries(table, hidden_near, chosen)
     build_columns(slots, table, shifted, columns)
     weight_sums(masked, columns, sums)
@@ -534,7 +536,11 @@
     forward(0)
     total2.planes()
     total1.column()
-    transpose(weights1)
+    back_weights(weights1, back)
+    faces[...] = jnp.zeros_like(faces)
+    for t in range(B):
+        transpose(t)
+    add_own()
     gather_gradients(faces, chosen, out2)
     returns2.start()
     total2.column()
@@ -613,7 +619,7 @@
         in_specs=[HBM_SPEC] * 7,
         out_specs=[VMEM_SPEC] * 3,
         scratch_shapes=[pltpu.VMEM(dims, dtype) for dims, dtype in SCRATCH]
-        + [dma((2, 2, 6)), dma((2, 2, 6)), dma((2, 5)), dma((2, 5)), dma((7,)), pltpu.SMEM((B, 27), jnp.int32), pltpu.SMEM((4, 3), jnp.int32)] + 2 * sum_scratch(nz, nxy),
+        + [dma((2, 3, 6)), dma((2, 2, 6)), dma((2, 5)), dma((2, 5)), dma((7,)), pltpu.SMEM((B, 27), jnp.int32), pltpu.SMEM((4, 3), jnp.int32)] + 2 * sum_scratch(nz, nxy),
         compiler_params=pltpu.CompilerParams(
             collective_id=0, has_side_effects=True, vmem_limit_bytes=VMEM_LIMIT
         ),

time: 64.7 us -> 64.5 us (level)
  no operation moved by 1% of the time
where the time goes in v7:
time: 64.5 us; the launch traced here: 64.4 us
  Pallas kernels  63.7 us (99%)
    pallas_call x1, Pallas kernels, local(): pl.pallas_call(functools.partial(main_kernel, nz, nxy), out_shape=[blocks...  61.6 us
    pallas_call x1, Pallas kernels, local(): pl.pallas_call(functools.partial(last_kernel, scale), out_shape=[blocks,...  2.15 us

profile of v7, /device:TPU:1, one launch (start us, length us, event | category | flops | bytes accessed | tf_op | source)
XLA Modules:
  0.0 64.4 jit_solution(2261207046391788349)
XLA Ops:
  0.6 61.6 %shard_map.102 = (bf16[2,96,512]{2,1,0:T(8,128)(2,1)S(1)}, bf16[2,96,512]{2,1,0:T(8,128)(2,1)S(1)}, bf16[4096,128]{1,0:T(8,128)(2,1)S(1)}) custom-call(s32[2,27]{1,0:T(2,128)} %far_slots.1, s32[4,3]{1,0:T(4,128)} %bitcast.3, bf16[2,96,512]{2,1,0:T(8,128)(2,1)} %far_features.1, s32[2,512]{1,0:T(2,128)} %far_occupancy.1, bf16[2,96,512]{2,1,0:T(8,128)(2,1)} %far_out_grad.1, ...), custom_call_target="tpu_custom_call" | custom-call | tf_op jit(solution)/shard_map/pallas_call | solution.py:616
  62.2 2.2 %shard_map.103 = (bf16[2,96,512]{2,1,0:T(8,128)(2,1)}, bf16[2,96,512]{2,1,0:T(8,128)(2,1)}, f32[27,96,96]{2,1,0:T(8,128)}, f32[27,96,96]{2,1,0:T(8,128)}) custom-call(bf16[4096,128]{1,0:T(8,128)(2,1)S(1)} %get-tuple-element.7.packed, bf16[2,96,512]{2,1,0:T(8,128)(2,1)S(1)} %get-tuple-element.8.output, bf16[2,96,512]{2,1,0:T(8,128)(2,1)S(1)} %get-tuple-element.9.grad), custom_call_target="tpu_custom_call" | custom-call | tf_op jit(solution)/shard_map/pallas_call | solution.py:628

commit v8 on v7

--- a/solution.py
+++ b/solution.py
@@ -25,7 +25,7 @@
 HALF = 1024
 ROWS = 2 * HALF
 WG = 27 * C
-QUARTER = WG // 4
+SPLIT = ((0, 14), (14, 27))
 MESSAGE = 2 * TIGHT + 16
 FACES = 384
 TIGHT_FACES = FACES * 3 // 4
@@ -196,37 +196,41 @@
     lax.fori_loop(0, EMPTY, one, 0)
 
 
-def weight_sums(left, columns, out):
-    for o in range(0, 27, 3):
-        sums = jnp.dot(left[...], columns[:, o * L : (o + 3) * L], preferred_element_type=F32)
-        for i in range(3):
-            row = (o + i) * C
-            out[row : row + C] = sums[0:C, i * L : (i + 1) * L]
-
-
-def pack_sums(sums, packed, at):
-    last = sums[3 * QUARTER : WG]
-    lane = lax.broadcasted_iota(jnp.int32, (QUARTER, L), 1)
-    for i in range(3):
-        moved = pltpu.roll(last, C - 32 * i, 1)
-        rows = slice(i * QUARTER, (i + 1) * QUARTER)
-        packed[at + i * QUARTER : at + (i + 1) * QUARTER] = jnp.where(lane < C, sums[rows], moved)
-    packed[at + 3 * QUARTER : at + ROWS] = jnp.zeros((ROWS - 3 * QUARTER, L), F32)
+def half_sums(left, columns, sums, packed, h):
+    start, end = SPLIT[h]
+    for o in range(start, end, 3):
+        count = min(3, end - o)
+        part = jnp.dot(left[...], columns[:, o * L : (o + count) * L], preferred_element_type=F32)
+        for i in range(count):
+            sums[(o + i) * C : (o + i + 1) * C] = part[0:C, i * L : (i + 1) * L]
+    size = (end - start) * C * 3 // 4
+    packed[h * HALF : h * HALF + size] = squeeze(sums[start * C : end * C])
+    packed[h * HALF + size : (h + 1) * HALF] = jnp.zeros((HALF - size, L), F32)
+
+
+def weight_sums(n, left, columns, sums, packed, total):
+    for mine in (False, True):
+        for core in range(2):
+            half = core if mine else 1 - core
+
+            @pl.when(n == core)
+            def _():
+                half_sums(left, columns, sums, packed, half)
+
+        if not mine:
+            total.cores()
 
 
 def last_kernel(scale, packed, output, grad, output_out, grad_out, first, second):
     output_out[...] = output[...]
     grad_out[...] = grad[...]
-    lane = lax.broadcasted_iota(jnp.int32, (QUARTER, L), 1)
     for i, out in enumerate((first, second)):
-        whole = packed[i * ROWS : (i + 1) * ROWS].astype(F32) * scale
-        last = jnp.zeros((QUARTER, L), F32)
-        for k in range(3):
-            part = whole[k * QUARTER : (k + 1) * QUARTER]
-            last = jnp.where(lane // 32 == k, pltpu.roll(part, 32 + 32 * k, 1), last)
-        for r in range(0, WG, 24):
-            part = whole[r : r + 24] if r < 3 * QUARTER else last[r - 3 * QUARTER : r - 3 * QUARTER + 24]
-            out[r // C, r % C : r % C + 24, :] = part[:, 0:C]
+        for h, (start, end) in enumerate(SPLIT):
+            size = (end - start) * C
+            at = i * ROWS + h * HALF
+            rows = stretch((packed[at : at + HALF].astype(F32) * scale)[0 : size * 3 // 4])
+            for r in range(0, size, 24):
+                out[start + r // C, r % C : r % C + 24, :] = rows[r : r + 24, 0:C]
 
 
 def send(source, dest, sems, peer):
@@ -445,9 +449,6 @@
         for i in range(4):
             rows = jnp.where(row == i, plan[i, g].astype(F32), rows)
         messages[g, 2 * TIGHT : MESSAGE] = rows.astype(BF16)
-    pl.semaphore_wait(pltpu.get_barrier_semaphore(), len(everyone))
-    for k in range(1 + B):
-        actives.start([messages.at[g] for g in range(3)], k)
 
     loads[3].wait()
     padded[...] = jnp.zeros_like(padded)
@@ -472,6 +473,9 @@
     loads[5].wait()
     back_weights(weights2, back)
     faces[...] = jnp.zeros_like(faces)
+    pl.semaphore_wait(pltpu.get_barrier_semaphore(), len(everyone))
+    for k in range(1 + B):
+        actives.start([messages.at[g] for g in range(3)], k)
     transpose(0)
     transpose(1)
     add_own()
@@ -511,9 +515,7 @@
         grad = grads[t].reshape(V, L) * slope[t]
         padded[t, 2:10, 2:10] = grad.reshape(8, 8, 8, L)
         pre[:, t * V : (t + 1) * V] = grad.T.astype(BF16)
-    weight_sums(pre, columns, sums)
-    pack_sums(sums, packed1, 0)
-    total1.cores()
+    weight_sums(n, pre, columns, sums, packed1, total1)
 
     for t in range(B):
         hiddens.forward(t)
@@ -522,9 +524,7 @@
         hiddens.settle(t)
     halo_entries(table, hidden_near, chosen)
     build_columns(slots, table, shifted, columns)
-    weight_sums(masked, columns, sums)
-    pack_sums(sums, packed2, 0)
-    total2.cores()
+    weight_sums(n, masked, columns, sums, packed2, total2)
 
     def forward(t):
         seen = occupancy[t : t + 1, :].astype(F32)

time: 64.5 us -> 64.5 us (level)
  no operation moved by 1% of the time
where the time goes in v8:
time: 64.5 us; the launch traced here: 64.4 us
  Pallas kernels  63.7 us (99%)
    pallas_call x1, Pallas kernels, local(): pl.pallas_call(functools.partial(main_kernel, nz, nxy), out_shape=[blocks...  61.6 us
    pallas_call x1, Pallas kernels, local(): pl.pallas_call(functools.partial(last_kernel, scale), out_shape=[blocks,...  2.15 us

profile of v8, /device:TPU:1, one launch (start us, length us, event | category | flops | bytes accessed | tf_op | source)
XLA Modules:
  0.0 64.4 jit_solution(6076543774074448363)
XLA Ops:
  0.6 61.6 %shard_map.102 = (bf16[2,96,512]{2,1,0:T(8,128)(2,1)S(1)}, bf16[2,96,512]{2,1,0:T(8,128)(2,1)S(1)}, bf16[4096,128]{1,0:T(8,128)(2,1)S(1)}) custom-call(s32[2,27]{1,0:T(2,128)} %far_slots.1, s32[4,3]{1,0:T(4,128)} %bitcast.3, bf16[2,96,512]{2,1,0:T(8,128)(2,1)} %far_features.1, s32[2,512]{1,0:T(2,128)} %far_occupancy.1, bf16[2,96,512]{2,1,0:T(8,128)(2,1)} %far_out_grad.1, ...), custom_call_target="tpu_custom_call" | custom-call | tf_op jit(solution)/shard_map/pallas_call | solution.py:616
  62.2 2.1 %shard_map.103 = (bf16[2,96,512]{2,1,0:T(8,128)(2,1)}, bf16[2,96,512]{2,1,0:T(8,128)(2,1)}, f32[27,96,96]{2,1,0:T(8,128)}, f32[27,96,96]{2,1,0:T(8,128)}) custom-call(bf16[4096,128]{1,0:T(8,128)(2,1)S(1)} %get-tuple-element.7.packed, bf16[2,96,512]{2,1,0:T(8,128)(2,1)S(1)} %get-tuple-element.8.output, bf16[2,96,512]{2,1,0:T(8,128)(2,1)S(1)} %get-tuple-element.9.grad), custom_call_target="tpu_custom_call" | custom-call | tf_op jit(solution)/shard_map/pallas_call | solution.py:628

commit v9 on v8

--- a/solution.py
+++ b/solution.py
@@ -540,13 +540,13 @@
     faces[...] = jnp.zeros_like(faces)
     for t in range(B):
         transpose(t)
-    add_own()
+    total2.column()
     gather_gradients(faces, chosen, out2)
     returns2.start()
-    total2.column()
+    total1.planes_back()
     returns2.join()
+    add_own()
     forward(1)
-    total1.planes_back()
     total2.planes_back()
     returns2.add(grads)
     for t in range(B):

time: 64.5 us -> 62.9 us (0.975)
  Pallas kernels: 63.7 us -> 62.2 us
    pallas_call x1, Pallas kernels: 61.6 us -> 60 us  [local(): pl.pallas_call(functools.partial(main_kernel, nz, nxy), out_shape=[blocks...]
where the time goes in v9:
time: 62.9 us; the launch traced here: 62.8 us
  Pallas kernels  62.2 us (99%)
  between operations  0.64 us (1%)
    pallas_call x1, Pallas kernels, local(): pl.pallas_call(functools.partial(main_kernel, nz, nxy), out_shape=[blocks...  60 us
    pallas_call x1, Pallas kernels, local(): pl.pallas_call(functools.partial(last_kernel, scale), out_shape=[blocks,...  2.15 us

profile of v9, /device:TPU:1, one launch (start us, length us, event | category | flops | bytes accessed | tf_op | source)
XLA Modules:
  0.0 62.8 jit_solution(6317148284484059048)
XLA Ops:
  0.6 60.0 %shard_map.102 = (bf16[2,96,512]{2,1,0:T(8,128)(2,1)S(1)}, bf16[2,96,512]{2,1,0:T(8,128)(2,1)S(1)}, bf16[4096,128]{1,0:T(8,128)(2,1)S(1)}) custom-call(s32[2,27]{1,0:T(2,128)} %far_slots.1, s32[4,3]{1,0:T(4,128)} %bitcast.3, bf16[2,96,512]{2,1,0:T(8,128)(2,1)} %far_features.1, s32[2,512]{1,0:T(2,128)} %far_occupancy.1, bf16[2,96,512]{2,1,0:T(8,128)(2,1)} %far_out_grad.1, ...), custom_call_target="tpu_custom_call" | custom-call | tf_op jit(solution)/shard_map/pallas_call | solution.py:616
  60.7 2.1 %shard_map.103 = (bf16[2,96,512]{2,1,0:T(8,128)(2,1)}, bf16[2,96,512]{2,1,0:T(8,128)(2,1)}, f32[27,96,96]{2,1,0:T(8,128)}, f32[27,96,96]{2,1,0:T(8,128)}) custom-call(bf16[4096,128]{1,0:T(8,128)(2,1)S(1)} %get-tuple-element.7.packed, bf16[2,96,512]{2,1,0:T(8,128)(2,1)S(1)} %get-tuple-element.8.output, bf16[2,96,512]{2,1,0:T(8,128)(2,1)S(1)} %get-tuple-element.9.grad), custom_call_target="tpu_custom_call" | custom-call | tf_op jit(solution)/shard_map/pallas_call | solution.py:628
